TPU v7x, 32 devices: a whole 2x2x4 slice. The times are simulated.
32 devices in a mesh: dom: 8 (over z, x), blk: 4 (over y, core).
Axes of the slice: x: 2, y: 2, z: 4, core: 2. Of those that a mesh axis runs over, the one named last changes fastest.
Arguments:
- displacement: float32 [4096, 96], P(('dom', 'blk')), may hold values from -6 to 6
- damage: float32 [4096, 96], P(('dom', 'blk')), may hold values from 0 to 0.95
- applied_load: float32 [4096, 96], P(('dom', 'blk')), may hold values from -300 to 300
- tangent: bfloat16 [4096, 5, 96, 96], P(('dom', 'blk')), may hold values from -0.625 to 0.625
- laplacian: bfloat16 [4096, 5, 96, 96], P(('dom', 'blk')), may hold values from -0.25 to 0.25
- block_columns: int32 [4096, 5], P(('dom', 'blk')), may hold values from 0 to 1023, as said below
- send_lists: int32 [8, 2, 256], P('dom'), may hold values from -1 to 511, as said below
- hist_mech: float32 [4096, 27, 96], P(('dom', 'blk')), may hold values from 0 to 200
- mech_dest: int32 [4096], P(('dom', 'blk')), may hold values from 0 to 4095, as said below
- strain_matrix: float32 [27, 96, 96], replicated, may hold values from -0.625 to 0.625
- quad_weight: float32 [27], replicated, may hold values from 0.018518519 to 0.055555556
Outputs:
- mech_out: float32 [4096, 96], P(('dom', 'blk'))
- dmg_out: float32 [4096, 96], P(('dom', 'blk'))
- norms: float32 [2], replicated
Inputs may be any that keep to these rules, and one draw needn't show every extreme that they name: mech_dest is a permutation of the block rows. The 128 rows of one device go to at most 5 rows of any one device (itself included), and that many are reached in every draw. `send_lists`: -1 marks an unused slot; used slots come first and name distinct rows of the group, numbered within the group. Group 0 lists nothing for the group below and the last group nothing for the group above. Some list uses all 256 slots. `block_columns`: entries of the ghost parts of the extended numbering name only used slots of the neighbours' lists, never those of a missing neighbour, and every used slot is named by some block row of the receiving group.
All inputs are finite; a program needn't handle non-finite values.
Results may differ from a plain program's by a relative error of at most 0.00047.
Values may be sent and summed in bfloat16 or wider, within the bound.
No kernel may reach another device: no remote copies, remote signals or barrier semaphores. Data moves between devices by JAX's collectives and lax.ppermute only.
A program may use at most 128 MiB of HBM per device.

v0:
```python
import functools

import jax
import jax.numpy as jnp
from jax import lax
from jax.experimental import pallas as pl
from jax.experimental.pallas import tpu as pltpu
from jax.sharding import PartitionSpec as P

F32 = jnp.float32
BF16 = jnp.bfloat16
FILL = 10**10
VMEM_LIMIT = 4 * 1024 * 1024


def dot(a, b):
    return lax.dot_general(a, b, (((1,), (0,)), ((), ())), preferred_element_type=F32)


def dot_nt(a, b):
    return lax.dot_general(a, b, (((1,), (1,)), ((), ())), preferred_element_type=F32)


def split2(x):
    hi = x.astype(BF16)
    lo = (x - hi.astype(F32)).astype(BF16)
    return hi, lo


def split3(x):
    hi = x.astype(BF16)
    rest = x - hi.astype(F32)
    mid = rest.astype(BF16)
    lo = (rest - mid.astype(F32)).astype(BF16)
    return hi, mid, lo


def one_hot(cond):
    return jnp.where(cond, 1.0, 0.0).astype(BF16)


def iota(shape, dim):
    return lax.broadcasted_iota(jnp.int32, shape, dim)


def parcel_shape(devices, values, lanes):
    return (devices, -(-values // (4 * lanes)), 4, lanes)


def pack(hot, table, out, tail=0.0):
    devices, groups, _, lanes = out.shape
    hi, lo = split2(table)
    moved = dot_nt(hot, hi) + dot_nt(hot, lo)
    cap, width = moved.shape[0] // devices, moved.shape[1]
    rows = [moved[k * devices : (k + 1) * devices] for k in range(cap)]
    rows.append(jnp.zeros((devices, groups * 4 * lanes - cap * width), F32))
    flat = jnp.concatenate(rows, axis=1)
    for j in range(groups * 4):
        line = flat[:, j * lanes : (j + 1) * lanes]
        out[:, j // 4, j % 4, :] = line + tail if j == groups * 4 - 1 else line


def unpack(hot, got, width):
    devices, groups, _, lanes = got.shape
    flat = jnp.concatenate([got[:, j // 4, j % 4, :] for j in range(groups * 4)], axis=1)
    cap = hot.shape[0] // devices
    rows = jnp.concatenate([flat[:, k * width : (k + 1) * width] for k in range(cap)], axis=0)
    blank = jnp.zeros((cap * devices, -width % lanes), F32)
    tall = jnp.concatenate([rows, blank], axis=1).T[:width]
    hi, lo = split2(tall)
    return dot(hi, hot) + dot(lo, hot)


def asked_hot(request, cap):
    devices, _, lanes = request.shape
    slots = request[:, 0, :]
    lane = iota((devices, lanes), 1).astype(F32)
    hots = [one_hot(lane == slots[:, k : k + 1] - 1.0) for k in range(cap)]
    return jnp.concatenate(hots, axis=0)


def asking_hot(bucket, cap, devices):
    place = iota((devices, bucket.shape[1]), 0) * cap
    hots = [one_hot(place + k == bucket[...]) for k in range(cap)]
    return jnp.concatenate(hots, axis=0)


def root_of(damage):
    return jnp.sqrt((1.0 - damage) ** 2 + 0.001)


def fields_kernel(stacked, fields):
    width = stacked.shape[0] // 2
    dmg = stacked[width:, :]
    fields[:width, :] = (root_of(dmg) * stacked[:width, :]).astype(BF16)
    fields[width:, :] = dmg.astype(BF16)


def request_kernel(cap, dest, request, bucket):
    devices, _, lanes = request.shape
    d = dest[...]
    owner = d // lanes
    slot = d - owner * lanes
    square = jnp.broadcast_to(owner.astype(F32), (lanes, lanes))
    diag = iota((lanes, lanes), 0) == iota((lanes, lanes), 1)
    column = jnp.sum(jnp.where(diag, square, 0.0), axis=1, keepdims=True)
    before = iota((lanes, lanes), 0) < iota((lanes, lanes), 1)
    same = (column == square) & before
    rank = jnp.sum(jnp.where(same, 1.0, 0.0), axis=0, keepdims=True).astype(jnp.int32)
    bucket[...] = owner * cap + rank
    wanted = jnp.where(iota((devices, lanes), 0) == owner, (slot + 1).astype(F32), 0.0)
    ranks = one_hot(iota((lanes, lanes), 0) == rank)
    request[...] = dot_nt(wanted.astype(BF16), ranks)[:, None, :]


def pick_kernel(group, lists, out):
    parts = group.shape[0]
    table = jnp.concatenate([group[j] for j in range(parts)], axis=1)
    odd = lax.axis_index("blk") % 2
    row = jnp.where(odd == 0, lists[1:2, :], lists[0:1, :])
    hot = one_hot(iota((table.shape[1], row.shape[1]), 0) == row)
    out[...] = dot(table, hot).astype(BF16)


def total_of(x):
    line = jnp.sum(x * x, axis=0, keepdims=True)
    return jnp.sum(line, axis=1, keepdims=True)


def source_kernel(cap, got, bucket, hist, smat, weight, mech_total, out):
    quads, width, lanes = hist.shape
    hot = asking_hot(bucket, cap, got.shape[0])
    held = unpack(hot, got, 3 * width)
    d_hi, d_lo = split2(held[:width])
    acc = jnp.zeros((width, lanes), F32)
    for q in range(quads):
        s_hi, s_lo = split2(smat[q])
        strain = dot(s_hi, d_hi) + (dot(s_hi, d_lo) + dot(s_lo, d_hi))
        acc = acc + weight[0, q] * jnp.maximum(hist[q], 0.5 * strain * strain)
    dmg_res = held[width : 2 * width] + 2.0 * acc * held[2 * width :]
    spare = iota((1, lanes), 1) - (lanes - 2)
    tail = jnp.where(spare == 0, mech_total[...], 0.0)
    tail = jnp.where(spare == 1, total_of(dmg_res), tail)
    pack(hot, dmg_res, out, tail)


def matvec_kernel(
    cap,
    group,
    mine_ghost,
    other_ghost,
    columns,
    tan,
    lap,
    request,
    disp,
    damage,
    load,
    mech,
    mech_total,
    parcels,
    left,
    near,
    diff,
):
    kblk, rows, width, lanes = tan.shape
    parts = group.shape[0]
    depth = kblk * width
    ghost = mine_ghost.shape[1]
    table = jnp.concatenate(
        [group[j] for j in range(parts)] + [mine_ghost[...], other_ghost[...]], axis=1
    )
    wanted = jnp.concatenate([columns[k : k + 1, :] for k in range(kblk)], axis=1)
    odd = lax.axis_index("blk") % 2
    own = parts * lanes
    starts = (0, own + odd * ghost, own + ghost - odd * ghost)
    hots = [
        one_hot(iota((size, kblk * lanes), 0) + start == wanted)
        for size, start in zip((own, ghost, ghost), starts)
    ]
    hot = jnp.concatenate(hots, axis=0)
    found = dot(table, hot)
    tall = []
    for field in range(2):
        cut = [
            found[field * width : (field + 1) * width, k * lanes : (k + 1) * lanes]
            for k in range(kblk)
        ]
        tall.append(jnp.concatenate(cut, axis=0))
    left[...] = tall[0].T.astype(BF16)
    near[...] = tall[1]
    lane = iota((8, 2 * lanes), 1) % lanes
    mine = iota((8, 2 * lanes), 0) == lane % 8

    @pl.loop(0, rows // 8)
    def _(step):
        place = pl.ds(pl.multiple_of(step * 8, 8), 8)
        lines = []
        for r in range(0, 8, 2):
            pair = [tan[:, step * 8 + r + j].reshape(depth, lanes) for j in range(2)]
            full = dot(left[...], jnp.concatenate(pair, axis=1))
            kept = full[:8]
            for g in range(1, lanes // 8):
                kept = jnp.where(lane // 8 == g, full[g * 8 : g * 8 + 8], kept)
            line = jnp.sum(jnp.where(mine, kept, 0.0), axis=0, keepdims=True)
            lines += [line[:, :lanes], line[:, lanes:]]
        mech[place, :] = jnp.concatenate(lines, axis=0)
        acc = [jnp.zeros((8, lanes), F32) for _ in range(8)]
        for k in range(kblk):
            for c in range(0, width, 16):
                base = k * width + c
                lo = near[base : base + 8, :]
                hi = near[base + 8 : base + 16, :]
                for r in range(8):
                    block = lap[k, step * 8 + r, c : c + 16, :].astype(F32)
                    acc[r] = acc[r] + (block[:8] * lo + block[8:] * hi)
        sums = [jnp.sum(a, axis=0, keepdims=True) for a in acc]
        diff[place, :] = jnp.concatenate(sums, axis=0)


    d = damage[...]
    mech_res = root_of(d) * mech[...] - load[...]
    mech[...] = mech_res
    mech_total[...] = jnp.broadcast_to(total_of(mech_res), mech_total.shape)
    table = jnp.concatenate([disp[...], diff[...] + d, d - 1.0], axis=0)
    pack(asked_hot(request, cap), table, parcels)


def scale_kernel(cap, entries, got, request, mech, mech_out, dmg_out, norms):
    width, lanes = mech.shape
    last = got[:, got.shape[1] - 1, 3, :]
    total = jnp.sum(last, axis=0, keepdims=True)[:, lanes - 2 :]
    norm = jnp.sqrt(total / entries + 1e-06)
    mech_out[...] = mech[...] / norm[:, 0:1]
    dmg_out[...] = unpack(asked_hot(request, cap), got, width) / norm[:, 1:2]
    norms[...] = norm


VM = pl.BlockSpec(memory_space=pltpu.VMEM)
SM = pl.BlockSpec(memory_space=pltpu.SMEM)


def call(body, outs, ins, scratch=(), flops=0, nbytes=0, specs=None):
    one = not isinstance(outs, (list, tuple))
    return pl.pallas_call(
        body,
        out_shape=outs,
        in_specs=specs or [VM] * ins,
        out_specs=VM if one else [VM] * len(outs),
        scratch_shapes=list(scratch),
        compiler_params=pltpu.CompilerParams(vmem_limit_bytes=VMEM_LIMIT),
        cost_estimate=pl.CostEstimate(flops=flops, bytes_accessed=nbytes, transcendentals=0),
    )


def sds(shape, dtype=F32):
    return jax.ShapeDtypeStruct(shape, dtype)


def swap(x, axes):
    return lax.all_to_all(x, axes, split_axis=0, concat_axis=0, tiled=True)


def on_device(
    displacement,
    damage,
    applied_load,
    tangent,
    laplacian,
    block_columns,
    send_lists,
    hist_mech,
    mech_dest,
    strain_matrix,
    quad_weight,
):
    lanes, width = displacement.shape
    kblk = tangent.shape[1]
    quads = hist_mech.shape[1]
    ghost = send_lists.shape[2]
    both = ("dom", "blk")
    devices = lax.axis_size(both)
    groups = lax.axis_size("dom")
    disp_t = displacement.T
    dmg_t = damage.T
    load_t = applied_load.T
    tan_t = jnp.transpose(tangent, (1, 2, 3, 0))
    lap_t = jnp.transpose(laplacian, (1, 2, 3, 0))
    hist_t = jnp.transpose(hist_mech, (1, 2, 0))
    cols_t = block_columns.T

    cap = lanes // devices + 1
    stacked = jnp.concatenate([disp_t, dmg_t], axis=0)
    with jax.named_scope("fields"):
        fields = call(fields_kernel, sds(stacked.shape, BF16), 1, flops=FILL)(stacked)
    group = lax.all_gather(fields, "blk", axis=0, tiled=False)
    with jax.named_scope("picks"):
        picked = call(pick_kernel, sds((2 * width, ghost), BF16), 2, flops=20 * FILL)(
            group, send_lists[0]
        )
    picked, mech_dest = lax.optimization_barrier((picked, mech_dest))
    with jax.named_scope("requests"):
        request, bucket = call(
            functools.partial(request_kernel, cap),
            [sds((devices, 1, lanes)), sds((1, lanes), jnp.int32)],
            1,
            flops=FILL,
        )(mech_dest[None, :])
    wanted = swap(request, both)
    blocks = lax.axis_size("blk")
    everyone = [(a, b) for a in range(groups) for b in range(blocks)]
    hop = [(a * blocks + b, (a + 1 - b % 2 * 2) * blocks + b) for a, b in everyone]
    hop = [(i, j) for i, j in hop if 0 <= j < groups * blocks]
    side = [(b, b ^ 1) for b in range(blocks)]
    mine_ghost = lax.ppermute(picked, both, hop)
    mine_ghost, wanted = lax.optimization_barrier((mine_ghost, wanted))
    other_ghost = lax.ppermute(mine_ghost, "blk", side)
    with jax.named_scope("matvec"):
        mech, mech_total, parcels = call(
            functools.partial(matvec_kernel, cap),
            [
                sds((width, lanes)),
                sds((1, lanes)),
                sds(parcel_shape(devices, 3 * cap * width, lanes)),
            ],
            10,
            [
                pltpu.VMEM((lanes, kblk * width), BF16),
                pltpu.VMEM((kblk * width, lanes), F32),
                pltpu.VMEM((width, lanes), F32),
            ],
            flops=FILL,
        )(group, mine_ghost, other_ghost, cols_t, tan_t, lap_t, wanted, disp_t, dmg_t, load_t)
    asked = swap(parcels, both)
    with jax.named_scope("source"):
        answer = call(
            functools.partial(source_kernel, cap),
            sds(parcel_shape(devices, cap * width + 2, lanes)),
            6,
            flops=FILL,
            specs=[VM, VM, VM, VM, SM, VM],
        )(asked, bucket, hist_t, strain_matrix, quad_weight[None, :], mech_total)
    got = swap(answer, both)
    with jax.named_scope("scale"):
        mech_out, dmg_out, norms = call(
            functools.partial(scale_kernel, cap, float(lanes * width * devices)),
            [sds((width, lanes)), sds((width, lanes)), sds((1, 2))],
            3,
        )(got, wanted, mech)
    return mech_out.T, dmg_out.T, norms[0]


def solution(mesh):
    rows = P(("dom", "blk"))
    in_specs = (rows,) * 6 + (P("dom"),) + (rows,) * 2 + (P(), P())
    out_specs = (rows, rows, P())
    return jax.shard_map(
        on_device, mesh=mesh, in_specs=in_specs, out_specs=out_specs, check_vma=False
    )
```

profile of v0, /device:TPU:0, one launch (start us, length us, event | category | flops | bytes accessed | tf_op | source)
XLA Modules:
  0.0 55.6 jit_solution(13795728723274611290)
XLA Ops:
  0.6 0.8 %pad_maximum_fusion.stacked = f32[192,128]{1,0:T(8,128)S(1)} fusion(f32[96,128]{1,0:T(8,128)} %bitcast.16, f32[96,128]{1,0:T(8,128)} %bitcast.18), kind=kLoop, calls=%fused_computation | loop fusion | flops 24576 | bytes 196608 | tf_op jit(solution)/shard_map/concatenate | solution.py:293
  1.5 6.9 %all-gather = bf16[768,128]{1,0:T(8,128)(2,1)S(1)} all-gather(bf16[192,128]{1,0:T(8,128)(2,1)S(1)} %fields.1), channel_id=2, replica_groups=mesh['dom'=8,'blk'=4] {'blk'}, dimensions={0}, use_global_device_ids=true | all-gather | bytes 245760 | tf_op jit(solution)/shard_map/all_gather | solution.py:296
  8.4 0.0 copy-done.8
  8.4 0.2 picks.1
  8.6 3.6 %collective-permute-start = (bf16[192,256]{1,0:T(8,128)(2,1)S(1)}, bf16[192,256]{1,0:T(8,128)(2,1)S(1)}, u32[]{:S(2)}, u32[]{:S(2)}) collective-permute-start(bf16[192,256]{1,0:T(8,128)(2,1)S(1)} %picks.1), channel_id=1, source_target_pairs={{0,4},{2,6},{4,8},{5,1},{6,10},{7,3},{8,12},{9,5},{10,14},{11,7},{... | collective-permute-start | bytes 294920 | tf_op jit(solution)/shard_map/ppermute | solution.py:315
  12.2 0.0 copy-done.9
  12.2 0.0 copy-start
  12.2 0.0 copy-start.1
  12.2 0.0 copy-start.2
  12.2 0.0 copy-start.3
  12.3 0.0 copy-start.6
  12.3 0.0 copy-start.7
  12.3 0.3 requests.1
  12.6 11.9 %all_to_all.15.request = f32[32,1,128]{2,1,0:T(1,128)S(1)} all-to-all(f32[32,1,128]{2,1,0:T(1,128)S(1)} %get-tuple-element.17), channel_id=1, replica_groups=mesh['dom'=8,'blk'=4] {'dom','blk'}, dimensions={0} | all-to-all | bytes 32768 | tf_op jit(solution)/shard_map/all_to_all | solution.py:261
  24.4 0.0 collective-permute-done.mine_ghost
  24.4 0.0 collective-permute-start.1
  24.4 1.3 %collective-permute-done.1.other_ghost = bf16[192,256]{1,0:T(8,128)(2,1)S(1)} collective-permute-done((bf16[192,256]{1,0:T(8,128)(2,1)S(1)}, bf16[192,256]{1,0:T(8,128)(2,1)S(1)}, u32[]{:S(2)}, u32[]{:S(2)}) %collective-permute-start.1) | collective-permute-done | bytes 98336 | tf_op jit(solution)/shard_map/ppermute | solution.py:317
  25.7 0.0 copy-done
  25.7 0.0 copy-done.1
  25.7 0.0 copy-done.2
  25.8 0.0 copy-done.3
  25.8 0.0 copy-done.6
  25.8 0.0 copy-start.4
  25.8 0.0 copy-start.5
  25.8 0.0 copy-start.10
  25.8 6.3 %matvec.1 = (f32[96,128]{1,0:T(8,128)S(1)}, f32[1,128]{1,0:T(1,128)S(1)}, f32[32,3,4,128]{3,2,1,0:T(4,128)S(1)}) custom-call(bf16[4,192,128]{2,1,0:T(8,128)(2,1)S(1)} %bitcast.15, bf16[192,256]{1,0:T(8,128)(2,1)S(1)} %collective-permute-done.mine_ghost, bf16[192,256]{1,0:T(8,128)(2,1)S(1)} %collective-permute-done.1.other_ghost, s32[5,128]{1,0:T(8,128)S(1)} %bitcast.24, ...), custom_call_target="tpu_custom_call" | custom-call | flops 10000000000 | tf_op jit(solution)/shard_map/matvec/pallas_call | solution.py:319
  32.1 10.6 %all_to_all.16.got = f32[32,3,4,128]{3,2,1,0:T(4,128)S(1)} all-to-all(f32[32,3,4,128]{3,2,1,0:T(4,128)S(1)} %get-tuple-element.20), channel_id=1, replica_groups=mesh['dom'=8,'blk'=4] {'dom','blk'}, dimensions={0} | all-to-all | bytes 393216 | tf_op jit(solution)/shard_map/all_to_all | solution.py:261
  42.7 0.0 copy-done.4
  42.7 0.0 copy-done.10
  42.7 2.0 %source.1 = f32[32,1,4,128]{3,2,1,0:T(4,128)S(1)} custom-call(f32[32,3,4,128]{3,2,1,0:T(4,128)S(1)} %all_to_all.16.got, s32[1,128]{1,0:T(1,128)S(1)} %get-tuple-element.21.bucket, f32[27,96,128]{2,1,0:T(8,128)S(1)} %bitcast.22, f32[27,96,96]{2,1,0:T(8,128)S(1)} %copy-done.5, f32[1,27]{1,0:T(1,128)S(1)} %bitcast.27, f32[1,128]{1,0:T(1,128)S(1)} %get-tuple-element.22.mech_total), custom_call_target="tpu_custom_call" | custom-call | flops 10000000000 | tf_op jit(solution)/shard_map/source/pallas_call | solution.py:336
  44.7 9.8 %all_to_all.17.got = f32[32,1,4,128]{3,2,1,0:T(4,128)S(1)} all-to-all(f32[32,1,4,128]{3,2,1,0:T(4,128)S(1)} %source.1), channel_id=1, replica_groups=mesh['dom'=8,'blk'=4] {'dom','blk'}, dimensions={0} | all-to-all | bytes 131072 | tf_op jit(solution)/shard_map/all_to_all | solution.py:261
  54.5 1.1 %scale.1 = (f32[96,128]{1,0:T(8,128)}, f32[96,128]{1,0:T(8,128)}, f32[1,2]{1,0:T(1,128)}) custom-call(f32[32,1,4,128]{3,2,1,0:T(4,128)S(1)} %all_to_all.17.got, f32[32,1,128]{2,1,0:T(1,128)S(1)} %all_to_all.15.request, f32[96,128]{1,0:T(8,128)S(1)} %get-tuple-element.23.mech), custom_call_target="tpu_custom_call" | custom-call | tf_op jit(solution)/shard_map/scale/pallas_call | solution.py:345
  (5 shorter events, 0.0 us)
Async XLA Ops:
  1.5 6.9 %copy-start.8 = (s32[1,2,256]{2,1,0:T(2,128)S(1)}, s32[1,2,256]{2,1,0:T(2,128)}, u32[]{:S(2)}) copy-start(s32[1,2,256]{2,1,0:T(2,128)} %param.17) | copy-start | bytes 6148
  8.4 3.8 %copy-start.9 = (s32[128]{0:T(128)S(1)}, s32[128]{0:T(128)}, u32[]{:S(2)}) copy-start(s32[128]{0:T(128)} %param.19) | copy-start | bytes 1540
  8.6 15.8 %collective-permute-start = (bf16[192,256]{1,0:T(8,128)(2,1)S(1)}, bf16[192,256]{1,0:T(8,128)(2,1)S(1)}, u32[]{:S(2)}, u32[]{:S(2)}) collective-permute-start(bf16[192,256]{1,0:T(8,128)(2,1)S(1)} %picks.1), channel_id=1, source_target_pairs={{0,4},{2,6},{4,8},{5,1},{6,10},{7,3},{8,12},{9,5},{10,14},{11,7},{... | collective-permute-start | bytes 294920 | tf_op jit(solution)/shard_map/ppermute | solution.py:315
  12.2 13.5 %copy-start = (f32[128,96]{0,1:T(8,128)S(1)}, f32[128,96]{0,1:T(8,128)}, u32[]{:S(2)}) copy-start(f32[128,96]{0,1:T(8,128)} %param.12) | copy-start | bytes 147460
  12.2 13.5 %copy-start.1 = (f32[128,96]{0,1:T(8,128)S(1)}, f32[128,96]{0,1:T(8,128)}, u32[]{:S(2)}) copy-start(f32[128,96]{0,1:T(8,128)} %param.11) | copy-start | bytes 147460
  12.2 13.5 %copy-start.2 = (bf16[128,5,96,96]{0,3,2,1:T(8,128)(2,1)S(1)}, bf16[128,5,96,96]{0,3,2,1:T(8,128)(2,1)}, u32[]{:S(2)}) copy-start(bf16[128,5,96,96]{0,3,2,1:T(8,128)(2,1)} %param.14) | copy-start | bytes 35389444
  12.2 13.5 %copy-start.3 = (bf16[128,5,96,96]{0,3,2,1:T(8,128)(2,1)S(1)}, bf16[128,5,96,96]{0,3,2,1:T(8,128)(2,1)}, u32[]{:S(2)}) copy-start(bf16[128,5,96,96]{0,3,2,1:T(8,128)(2,1)} %param.15) | copy-start | bytes 35389444
  12.3 13.5 %copy-start.6 = (f32[128,96]{0,1:T(8,128)S(1)}, f32[128,96]{0,1:T(8,128)}, u32[]{:S(2)}) copy-start(f32[128,96]{0,1:T(8,128)} %param.13) | copy-start | bytes 147460
  12.3 13.5 %copy-start.7 = (s32[128,5]{0,1:T(8,128)S(1)}, s32[128,5]{0,1:T(8,128)}, u32[]{:S(2)}) copy-start(s32[128,5]{0,1:T(8,128)} %param.16) | copy-start | bytes 7684
  24.4 1.3 %collective-permute-start.1 = (bf16[192,256]{1,0:T(8,128)(2,1)S(1)}, bf16[192,256]{1,0:T(8,128)(2,1)S(1)}, u32[]{:S(2)}, u32[]{:S(2)}) collective-permute-start(bf16[192,256]{1,0:T(8,128)(2,1)S(1)} %collective-permute-done.mine_ghost), channel_id=1, source_target_pairs={{0,1},{1,0},{2,3},{3,2},{4,5},{5,4},{6,7},{7,6},{8,9},{9,8},{10,11... | collective-permute-start | bytes 294920 | tf_op jit(solution)/shard_map/ppermute | solution.py:317
  25.8 16.9 %copy-start.4 = (f32[128,27,96]{0,2,1:T(8,128)S(1)}, f32[128,27,96]{0,2,1:T(8,128)}, u32[]{:S(2)}) copy-start(f32[128,27,96]{0,2,1:T(8,128)} %param.18) | copy-start | bytes 3981316
  25.8 16.9 %copy-start.5 = (f32[27,96,96]{2,1,0:T(8,128)S(1)}, f32[27,96,96]{2,1,0:T(8,128)}, u32[]{:S(2)}) copy-start(f32[27,96,96]{2,1,0:T(8,128)} %smat.1) | copy-start | bytes 2985988
  25.8 16.9 %copy-start.10 = (f32[27]{0:T(128)S(1)}, f32[27]{0:T(128)}, u32[]{:S(2)}) copy-start(f32[27]{0:T(128)} %param.21) | copy-start | bytes 328
where the time goes:
time: 55.9 us; the launch traced here: 55.6 us
  blocking collectives  39.2 us (70%)
  Pallas kernels  9.86 us (18%)
  starting transfers between devices  3.6 us (6%)
  waiting for transfers between devices  1.3 us (2%)
  other arithmetic  0.83 us (1%)
  between operations  0.79 us (1%)
    all_to_all x3, blocking collectives, swap(): return lax.all_to_all(x, axes, split_axis=0, concat_axis=0, tiled=True)  32.3 us
    all_gather x1, blocking collectives, on_device(): group = lax.all_gather(fields, 'blk', axis=0, tiled=False)  6.87 us
    pallas_call x1, Pallas kernels, on_device(): call(functools.partial(matvec_kernel, cap), [sds((width, lanes)), sds((1,...  6.29 us
    ppermute x1, starting transfers between devices, on_device(): mine_ghost = lax.ppermute(picked, both, hop)  3.6 us
    pallas_call x1, Pallas kernels, on_device(): call(functools.partial(source_kernel, cap), sds(parcel_shape(devices, cap...  1.98 us
    ppermute x1, waiting for transfers between devices, on_device(): other_ghost = lax.ppermute(mine_ghost, 'blk', side)  1.3 us
  transfers between devices with their start and end apart: 2, of which 1 were waited for; matrix products, arithmetic and copies ran while one was open for 0% of the time, Pallas kernels for 0%

commit v1 on v0

--- a/solution.py
+++ b/solution.py
@@ -131,11 +131,17 @@
     quads, width, lanes = hist.shape
     hot = asking_hot(bucket, cap, got.shape[0])
     held = unpack(hot, got, 3 * width)
-    d_hi, d_lo = split2(held[:width])
+    gap = jnp.zeros((lanes - width, lanes), F32)
+    d_hi, d_lo = split2(jnp.concatenate([held[:width], gap], axis=0))
+    upper = jnp.concatenate([d_hi, d_lo], axis=1)
+    lower = jnp.concatenate([d_hi, jnp.zeros_like(d_hi)], axis=1)
+    sides = jnp.concatenate([upper, lower], axis=0)
+    blank = jnp.zeros((width, lanes - width), F32)
     acc = jnp.zeros((width, lanes), F32)
     for q in range(quads):
-        s_hi, s_lo = split2(smat[q])
-        strain = dot(s_hi, d_hi) + (dot(s_hi, d_lo) + dot(s_lo, d_hi))
+        halves = split2(jnp.concatenate([smat[q], blank], axis=1))
+        full = dot(jnp.concatenate(halves, axis=1), sides)
+        strain = full[:, :lanes] + full[:, lanes:]
         acc = acc + weight[0, q] * jnp.maximum(hist[q], 0.5 * strain * strain)
     dmg_res = held[width : 2 * width] + 2.0 * acc * held[2 * width :]
     spare = iota((1, lanes), 1) - (lanes - 2)
@@ -195,28 +201,30 @@
     @pl.loop(0, rows // 8)
     def _(step):
         place = pl.ds(pl.multiple_of(step * 8, 8), 8)
-        lines = []
-        for r in range(0, 8, 2):
-            pair = [tan[:, step * 8 + r + j].reshape(depth, lanes) for j in range(2)]
-            full = dot(left[...], jnp.concatenate(pair, axis=1))
-            kept = full[:8]
-            for g in range(1, lanes // 8):
-                kept = jnp.where(lane // 8 == g, full[g * 8 : g * 8 + 8], kept)
-            line = jnp.sum(jnp.where(mine, kept, 0.0), axis=0, keepdims=True)
-            lines += [line[:, :lanes], line[:, lanes:]]
+        lines, sums = [], []
+        for half in range(0, 8, 4):
+            fulls = []
+            for r in range(half, half + 4, 2):
+                pair = [tan[:, step * 8 + r + j].reshape(depth, lanes) for j in range(2)]
+                fulls.append(dot(left[...], jnp.concatenate(pair, axis=1)))
+            acc = [jnp.zeros((8, lanes), F32) for _ in range(4)]
+            for k in range(kblk):
+                for c in range(0, width, 16):
+                    base = k * width + c
+                    lo = near[base : base + 8, :]
+                    hi = near[base + 8 : base + 16, :]
+                    for r in range(4):
+                        block = lap[k, step * 8 + half + r, c : c + 16, :].astype(F32)
+                        acc[r] = acc[r] + (block[:8] * lo + block[8:] * hi)
+            sums += [jnp.sum(a, axis=0, keepdims=True) for a in acc]
+            for full in fulls:
+                kept = full[:8]
+                for g in range(1, lanes // 8):
+                    kept = jnp.where(lane // 8 == g, full[g * 8 : g * 8 + 8], kept)
+                line = jnp.sum(jnp.where(mine, kept, 0.0), axis=0, keepdims=True)
+                lines += [line[:, :lanes], line[:, lanes:]]
         mech[place, :] = jnp.concatenate(lines, axis=0)
-        acc = [jnp.zeros((8, lanes), F32) for _ in range(8)]
-        for k in range(kblk):
-            for c in range(0, width, 16):
-                base = k * width + c
-                lo = near[base : base + 8, :]
-                hi = near[base + 8 : base + 16, :]
-                for r in range(8):
-                    block = lap[k, step * 8 + r, c : c + 16, :].astype(F32)
-                    acc[r] = acc[r] + (block[:8] * lo + block[8:] * hi)
-        sums = [jnp.sum(a, axis=0, keepdims=True) for a in acc]
         diff[place, :] = jnp.concatenate(sums, axis=0)
-
 
     d = damage[...]
     mech_res = root_of(d) * mech[...] - load[...]

time: 55.9 us -> 55.7 us (level)
  no operation moved by 1% of the time
where the time goes in v1:
time: 55.7 us; the launch traced here: 55.5 us
  blocking collectives  39.2 us (70%)
  Pallas kernels  9.69 us (17%)
  starting transfers between devices  3.6 us (6%)
  waiting for transfers between devices  1.3 us (2%)
  other arithmetic  0.83 us (1%)
  between operations  0.79 us (1%)
    all_to_all x3, blocking collectives, swap(): return lax.all_to_all(x, axes, split_axis=0, concat_axis=0, tiled=True)  32.3 us
    all_gather x1, blocking collectives, on_device(): group = lax.all_gather(fields, 'blk', axis=0, tiled=False)  6.87 us
    pallas_call x1, Pallas kernels, on_device(): call(functools.partial(matvec_kernel, cap), [sds((width, lanes)), sds((1,...  6.24 us
    ppermute x1, starting transfers between devices, on_device(): mine_ghost = lax.ppermute(picked, both, hop)  3.6 us
    pallas_call x1, Pallas kernels, on_device(): call(functools.partial(source_kernel, cap), sds(parcel_shape(devices, cap...  1.86 us
    ppermute x1, waiting for transfers between devices, on_device(): other_ghost = lax.ppermute(mine_ghost, 'blk', side)  1.3 us
  transfers between devices with their start and end apart: 2, of which 1 were waited for; matrix products, arithmetic and copies ran while one was open for 0% of the time, Pallas kernels for 0%

profile of v1, /device:TPU:0, one launch (start us, length us, event | category | flops | bytes accessed | tf_op | source)
XLA Modules:
  0.0 55.5 jit_solution(16016888212508362770)
XLA Ops:
  0.6 0.8 %pad_maximum_fusion.stacked = f32[192,128]{1,0:T(8,128)S(1)} fusion(f32[96,128]{1,0:T(8,128)} %bitcast.16, f32[96,128]{1,0:T(8,128)} %bitcast.18), kind=kLoop, calls=%fused_computation | loop fusion | flops 24576 | bytes 196608 | tf_op jit(solution)/shard_map/concatenate | solution.py:301
  1.5 6.9 %all-gather = bf16[768,128]{1,0:T(8,128)(2,1)S(1)} all-gather(bf16[192,128]{1,0:T(8,128)(2,1)S(1)} %fields.1), channel_id=2, replica_groups=mesh['dom'=8,'blk'=4] {'blk'}, dimensions={0}, use_global_device_ids=true | all-gather | bytes 245760 | tf_op jit(solution)/shard_map/all_gather | solution.py:304
  8.4 0.0 copy-done.8
  8.4 0.2 picks.1
  8.6 3.6 %collective-permute-start = (bf16[192,256]{1,0:T(8,128)(2,1)S(1)}, bf16[192,256]{1,0:T(8,128)(2,1)S(1)}, u32[]{:S(2)}, u32[]{:S(2)}) collective-permute-start(bf16[192,256]{1,0:T(8,128)(2,1)S(1)} %picks.1), channel_id=1, source_target_pairs={{0,4},{2,6},{4,8},{5,1},{6,10},{7,3},{8,12},{9,5},{10,14},{11,7},{... | collective-permute-start | bytes 294920 | tf_op jit(solution)/shard_map/ppermute | solution.py:323
  12.2 0.0 copy-done.9
  12.2 0.0 copy-start
  12.2 0.0 copy-start.1
  12.2 0.0 copy-start.2
  12.2 0.0 copy-start.3
  12.3 0.0 copy-start.6
  12.3 0.0 copy-start.7
  12.3 0.3 requests.1
  12.6 11.9 %all_to_all.15.request = f32[32,1,128]{2,1,0:T(1,128)S(1)} all-to-all(f32[32,1,128]{2,1,0:T(1,128)S(1)} %get-tuple-element.17), channel_id=1, replica_groups=mesh['dom'=8,'blk'=4] {'dom','blk'}, dimensions={0} | all-to-all | bytes 32768 | tf_op jit(solution)/shard_map/all_to_all | solution.py:269
  24.4 0.0 collective-permute-done.mine_ghost
  24.4 0.0 collective-permute-start.1
  24.4 1.3 %collective-permute-done.1.other_ghost = bf16[192,256]{1,0:T(8,128)(2,1)S(1)} collective-permute-done((bf16[192,256]{1,0:T(8,128)(2,1)S(1)}, bf16[192,256]{1,0:T(8,128)(2,1)S(1)}, u32[]{:S(2)}, u32[]{:S(2)}) %collective-permute-start.1) | collective-permute-done | bytes 98336 | tf_op jit(solution)/shard_map/ppermute | solution.py:325
  25.7 0.0 copy-done
  25.7 0.0 copy-done.1
  25.7 0.0 copy-done.2
  25.8 0.0 copy-done.3
  25.8 0.0 copy-done.6
  25.8 0.0 copy-done.7
  25.8 0.0 copy-start.4
  25.8 0.0 copy-start.5
  25.8 0.0 copy-start.10
  25.8 6.2 %matvec.1 = (f32[96,128]{1,0:T(8,128)S(1)}, f32[1,128]{1,0:T(1,128)S(1)}, f32[32,3,4,128]{3,2,1,0:T(4,128)S(1)}) custom-call(bf16[4,192,128]{2,1,0:T(8,128)(2,1)S(1)} %bitcast.15, bf16[192,256]{1,0:T(8,128)(2,1)S(1)} %collective-permute-done.mine_ghost, bf16[192,256]{1,0:T(8,128)(2,1)S(1)} %collective-permute-done.1.other_ghost, s32[5,128]{1,0:T(8,128)S(1)} %bitcast.24, ...), custom_call_target="tpu_custom_call" | custom-call | flops 10000000000 | tf_op jit(solution)/shard_map/matvec/pallas_call | solution.py:327
  32.1 10.6 %all_to_all.16.got = f32[32,3,4,128]{3,2,1,0:T(4,128)S(1)} all-to-all(f32[32,3,4,128]{3,2,1,0:T(4,128)S(1)} %get-tuple-element.20), channel_id=1, replica_groups=mesh['dom'=8,'blk'=4] {'dom','blk'}, dimensions={0} | all-to-all | bytes 393216 | tf_op jit(solution)/shard_map/all_to_all | solution.py:269
  42.7 0.0 copy-done.4
  42.7 1.9 %source.1 = f32[32,1,4,128]{3,2,1,0:T(4,128)S(1)} custom-call(f32[32,3,4,128]{3,2,1,0:T(4,128)S(1)} %all_to_all.16.got, s32[1,128]{1,0:T(1,128)S(1)} %get-tuple-element.21.bucket, f32[27,96,128]{2,1,0:T(8,128)S(1)} %bitcast.22, f32[27,96,96]{2,1,0:T(8,128)S(1)} %copy-done.5, f32[1,27]{1,0:T(1,128)S(1)} %bitcast.27, f32[1,128]{1,0:T(1,128)S(1)} %get-tuple-element.22.mech_total), custom_call_target="tpu_custom_call" | custom-call | flops 10000000000 | tf_op jit(solution)/shard_map/source/pallas_call | solution.py:344
  44.5 9.8 %all_to_all.17.got = f32[32,1,4,128]{3,2,1,0:T(4,128)S(1)} all-to-all(f32[32,1,4,128]{3,2,1,0:T(4,128)S(1)} %source.1), channel_id=1, replica_groups=mesh['dom'=8,'blk'=4] {'dom','blk'}, dimensions={0} | all-to-all | bytes 131072 | tf_op jit(solution)/shard_map/all_to_all | solution.py:269
  54.4 1.1 %scale.1 = (f32[96,128]{1,0:T(8,128)}, f32[96,128]{1,0:T(8,128)}, f32[1,2]{1,0:T(1,128)}) custom-call(f32[32,1,4,128]{3,2,1,0:T(4,128)S(1)} %all_to_all.17.got, f32[32,1,128]{2,1,0:T(1,128)S(1)} %all_to_all.15.request, f32[96,128]{1,0:T(8,128)S(1)} %get-tuple-element.23.mech), custom_call_target="tpu_custom_call" | custom-call | tf_op jit(solution)/shard_map/scale/pallas_call | solution.py:353
  (5 shorter events, 0.0 us)
Async XLA Ops:
  1.5 6.9 %copy-start.8 = (s32[1,2,256]{2,1,0:T(2,128)S(1)}, s32[1,2,256]{2,1,0:T(2,128)}, u32[]{:S(2)}) copy-start(s32[1,2,256]{2,1,0:T(2,128)} %param.17) | copy-start | bytes 6148
  8.4 3.8 %copy-start.9 = (s32[128]{0:T(128)S(1)}, s32[128]{0:T(128)}, u32[]{:S(2)}) copy-start(s32[128]{0:T(128)} %param.19) | copy-start | bytes 1540
  8.6 15.8 %collective-permute-start = (bf16[192,256]{1,0:T(8,128)(2,1)S(1)}, bf16[192,256]{1,0:T(8,128)(2,1)S(1)}, u32[]{:S(2)}, u32[]{:S(2)}) collective-permute-start(bf16[192,256]{1,0:T(8,128)(2,1)S(1)} %picks.1), channel_id=1, source_target_pairs={{0,4},{2,6},{4,8},{5,1},{6,10},{7,3},{8,12},{9,5},{10,14},{11,7},{... | collective-permute-start | bytes 294920 | tf_op jit(solution)/shard_map/ppermute | solution.py:323
  12.2 13.5 %copy-start = (f32[128,96]{0,1:T(8,128)S(1)}, f32[128,96]{0,1:T(8,128)}, u32[]{:S(2)}) copy-start(f32[128,96]{0,1:T(8,128)} %param.12) | copy-start | bytes 147460
  12.2 13.5 %copy-start.1 = (f32[128,96]{0,1:T(8,128)S(1)}, f32[128,96]{0,1:T(8,128)}, u32[]{:S(2)}) copy-start(f32[128,96]{0,1:T(8,128)} %param.11) | copy-start | bytes 147460
  12.2 13.5 %copy-start.2 = (bf16[128,5,96,96]{0,3,2,1:T(8,128)(2,1)S(1)}, bf16[128,5,96,96]{0,3,2,1:T(8,128)(2,1)}, u32[]{:S(2)}) copy-start(bf16[128,5,96,96]{0,3,2,1:T(8,128)(2,1)} %param.14) | copy-start | bytes 35389444
  12.2 13.5 %copy-start.3 = (bf16[128,5,96,96]{0,3,2,1:T(8,128)(2,1)S(1)}, bf16[128,5,96,96]{0,3,2,1:T(8,128)(2,1)}, u32[]{:S(2)}) copy-start(bf16[128,5,96,96]{0,3,2,1:T(8,128)(2,1)} %param.15) | copy-start | bytes 35389444
  12.3 13.5 %copy-start.6 = (f32[128,96]{0,1:T(8,128)S(1)}, f32[128,96]{0,1:T(8,128)}, u32[]{:S(2)}) copy-start(f32[128,96]{0,1:T(8,128)} %param.13) | copy-start | bytes 147460
  12.3 13.5 %copy-start.7 = (s32[128,5]{0,1:T(8,128)S(1)}, s32[128,5]{0,1:T(8,128)}, u32[]{:S(2)}) copy-start(s32[128,5]{0,1:T(8,128)} %param.16) | copy-start | bytes 7684
  24.4 1.3 %collective-permute-start.1 = (bf16[192,256]{1,0:T(8,128)(2,1)S(1)}, bf16[192,256]{1,0:T(8,128)(2,1)S(1)}, u32[]{:S(2)}, u32[]{:S(2)}) collective-permute-start(bf16[192,256]{1,0:T(8,128)(2,1)S(1)} %collective-permute-done.mine_ghost), channel_id=1, source_target_pairs={{0,1},{1,0},{2,3},{3,2},{4,5},{5,4},{6,7},{7,6},{8,9},{9,8},{10,11... | collective-permute-start | bytes 294920 | tf_op jit(solution)/shard_map/ppermute | solution.py:325
  25.8 16.9 %copy-start.4 = (f32[128,27,96]{0,2,1:T(8,128)S(1)}, f32[128,27,96]{0,2,1:T(8,128)}, u32[]{:S(2)}) copy-start(f32[128,27,96]{0,2,1:T(8,128)} %param.18) | copy-start | bytes 3981316
  25.8 16.9 %copy-start.5 = (f32[27,96,96]{2,1,0:T(8,128)S(1)}, f32[27,96,96]{2,1,0:T(8,128)}, u32[]{:S(2)}) copy-start(f32[27,96,96]{2,1,0:T(8,128)} %smat.1) | copy-start | bytes 2985988
  25.8 16.9 %copy-start.10 = (f32[27]{0:T(128)S(1)}, f32[27]{0:T(128)}, u32[]{:S(2)}) copy-start(f32[27]{0:T(128)} %param.21) | copy-start | bytes 328

commit v2 on v0

--- a/solution.py
+++ b/solution.py
@@ -131,11 +131,17 @@
     quads, width, lanes = hist.shape
     hot = asking_hot(bucket, cap, got.shape[0])
     held = unpack(hot, got, 3 * width)
-    d_hi, d_lo = split2(held[:width])
+    gap = jnp.zeros((lanes - width, lanes), F32)
+    d_hi, d_lo = split2(jnp.concatenate([held[:width], gap], axis=0))
+    upper = jnp.concatenate([d_hi, d_lo], axis=1)
+    lower = jnp.concatenate([d_hi, jnp.zeros_like(d_hi)], axis=1)
+    sides = jnp.concatenate([upper, lower], axis=0)
+    blank = jnp.zeros((width, lanes - width), F32)
     acc = jnp.zeros((width, lanes), F32)
     for q in range(quads):
-        s_hi, s_lo = split2(smat[q])
-        strain = dot(s_hi, d_hi) + (dot(s_hi, d_lo) + dot(s_lo, d_hi))
+        halves = split2(jnp.concatenate([smat[q], blank], axis=1))
+        full = dot(jnp.concatenate(halves, axis=1), sides)
+        strain = full[:, :lanes] + full[:, lanes:]
         acc = acc + weight[0, q] * jnp.maximum(hist[q], 0.5 * strain * strain)
     dmg_res = held[width : 2 * width] + 2.0 * acc * held[2 * width :]
     spare = iota((1, lanes), 1) - (lanes - 2)
@@ -144,28 +150,23 @@
     pack(hot, dmg_res, out, tail)
 
 
-def matvec_kernel(
+def laplacian_kernel(
     cap,
     group,
     mine_ghost,
     other_ghost,
     columns,
-    tan,
     lap,
     request,
     disp,
     damage,
-    load,
-    mech,
-    mech_total,
     parcels,
     left,
     near,
     diff,
 ):
-    kblk, rows, width, lanes = tan.shape
+    kblk, rows, width, lanes = lap.shape
     parts = group.shape[0]
-    depth = kblk * width
     ghost = mine_ghost.shape[1]
     table = jnp.concatenate(
         [group[j] for j in range(parts)] + [mine_ghost[...], other_ghost[...]], axis=1
@@ -178,8 +179,7 @@
         one_hot(iota((size, kblk * lanes), 0) + start == wanted)
         for size, start in zip((own, ghost, ghost), starts)
     ]
-    hot = jnp.concatenate(hots, axis=0)
-    found = dot(table, hot)
+    found = dot(table, jnp.concatenate(hots, axis=0))
     tall = []
     for field in range(2):
         cut = [
@@ -189,22 +189,9 @@
         tall.append(jnp.concatenate(cut, axis=0))
     left[...] = tall[0].T.astype(BF16)
     near[...] = tall[1]
-    lane = iota((8, 2 * lanes), 1) % lanes
-    mine = iota((8, 2 * lanes), 0) == lane % 8
 
     @pl.loop(0, rows // 8)
     def _(step):
-        place = pl.ds(pl.multiple_of(step * 8, 8), 8)
-        lines = []
-        for r in range(0, 8, 2):
-            pair = [tan[:, step * 8 + r + j].reshape(depth, lanes) for j in range(2)]
-            full = dot(left[...], jnp.concatenate(pair, axis=1))
-            kept = full[:8]
-            for g in range(1, lanes // 8):
-                kept = jnp.where(lane // 8 == g, full[g * 8 : g * 8 + 8], kept)
-            line = jnp.sum(jnp.where(mine, kept, 0.0), axis=0, keepdims=True)
-            lines += [line[:, :lanes], line[:, lanes:]]
-        mech[place, :] = jnp.concatenate(lines, axis=0)
         acc = [jnp.zeros((8, lanes), F32) for _ in range(8)]
         for k in range(kblk):
             for c in range(0, width, 16):
@@ -215,15 +202,46 @@
                     block = lap[k, step * 8 + r, c : c + 16, :].astype(F32)
                     acc[r] = acc[r] + (block[:8] * lo + block[8:] * hi)
         sums = [jnp.sum(a, axis=0, keepdims=True) for a in acc]
-        diff[place, :] = jnp.concatenate(sums, axis=0)
-
+        diff[pl.ds(pl.multiple_of(step * 8, 8), 8), :] = jnp.concatenate(sums, axis=0)
 
     d = damage[...]
-    mech_res = root_of(d) * mech[...] - load[...]
+    values = jnp.concatenate([disp[...], diff[...] + d, d - 1.0], axis=0)
+    pack(asked_hot(request, cap), values, parcels)
+
+
+def tangent_kernel(left, tan_hbm, damage, load, mech, mech_total, tan, sems):
+    kblk, rows, width, lanes = tan.shape
+    depth = kblk * width
+    steps = rows // 8
+
+    def piece(step):
+        place = pl.ds(pl.multiple_of(step * 8, 8), 8)
+        return pltpu.make_async_copy(tan_hbm.at[:, place], tan.at[:, place], sems.at[step])
+
+    @pl.loop(0, steps)
+    def _(step):
+        piece(step).start()
+
+    lane = iota((8, 2 * lanes), 1) % lanes
+    mine = iota((8, 2 * lanes), 0) == lane % 8
+
+    @pl.loop(0, steps)
+    def _(step):
+        piece(step).wait()
+        lines = []
+        for r in range(0, 8, 2):
+            pair = [tan[:, step * 8 + r + j].reshape(depth, lanes) for j in range(2)]
+            full = dot(left[...], jnp.concatenate(pair, axis=1))
+            kept = full[:8]
+            for g in range(1, lanes // 8):
+                kept = jnp.where(lane // 8 == g, full[g * 8 : g * 8 + 8], kept)
+            line = jnp.sum(jnp.where(mine, kept, 0.0), axis=0, keepdims=True)
+            lines += [line[:, :lanes], line[:, lanes:]]
+        mech[pl.ds(pl.multiple_of(step * 8, 8), 8), :] = jnp.concatenate(lines, axis=0)
+
+    mech_res = root_of(damage[...]) * mech[...] - load[...]
     mech[...] = mech_res
     mech_total[...] = jnp.broadcast_to(total_of(mech_res), mech_total.shape)
-    table = jnp.concatenate([disp[...], diff[...] + d, d - 1.0], axis=0)
-    pack(asked_hot(request, cap), table, parcels)
 
 
 def scale_kernel(cap, entries, got, request, mech, mech_out, dmg_out, norms):
@@ -237,10 +255,11 @@
 
 
 VM = pl.BlockSpec(memory_space=pltpu.VMEM)
+ANY = pl.BlockSpec(memory_space=pl.ANY)
 SM = pl.BlockSpec(memory_space=pltpu.SMEM)
 
 
-def call(body, outs, ins, scratch=(), flops=0, nbytes=0, specs=None):
+def call(body, outs, ins, scratch=(), flops=0, nbytes=0, specs=None, limit=VMEM_LIMIT):
     one = not isinstance(outs, (list, tuple))
     return pl.pallas_call(
         body,
@@ -248,7 +267,7 @@
         in_specs=specs or [VM] * ins,
         out_specs=VM if one else [VM] * len(outs),
         scratch_shapes=list(scratch),
-        compiler_params=pltpu.CompilerParams(vmem_limit_bytes=VMEM_LIMIT),
+        compiler_params=pltpu.CompilerParams(vmem_limit_bytes=limit),
         cost_estimate=pl.CostEstimate(flops=flops, bytes_accessed=nbytes, transcendentals=0),
     )
 
@@ -315,23 +334,29 @@
     mine_ghost = lax.ppermute(picked, both, hop)
     mine_ghost, wanted = lax.optimization_barrier((mine_ghost, wanted))
     other_ghost = lax.ppermute(mine_ghost, "blk", side)
-    with jax.named_scope("matvec"):
-        mech, mech_total, parcels = call(
-            functools.partial(matvec_kernel, cap),
+    with jax.named_scope("laplacian"):
+        parcels, left = call(
+            functools.partial(laplacian_kernel, cap),
             [
-                sds((width, lanes)),
-                sds((1, lanes)),
                 sds(parcel_shape(devices, 3 * cap * width, lanes)),
+                sds((lanes, kblk * width), BF16),
             ],
-            10,
-            [
-                pltpu.VMEM((lanes, kblk * width), BF16),
-                pltpu.VMEM((kblk * width, lanes), F32),
-                pltpu.VMEM((width, lanes), F32),
-            ],
+            8,
+            [pltpu.VMEM((kblk * width, lanes), F32), pltpu.VMEM((width, lanes), F32)],
             flops=FILL,
-        )(group, mine_ghost, other_ghost, cols_t, tan_t, lap_t, wanted, disp_t, dmg_t, load_t)
+        )(group, mine_ghost, other_ghost, cols_t, lap_t, wanted, disp_t, dmg_t)
     asked = swap(parcels, both)
+    with jax.named_scope("tangent"):
+        mech, mech_total = call(
+            tangent_kernel,
+            [sds((width, lanes)), sds((1, lanes))],
+            4,
+            [pltpu.VMEM(tan_t.shape, BF16), pltpu.SemaphoreType.DMA((width // 8,))],
+            flops=FILL,
+            specs=[VM, ANY, VM, VM],
+            limit=48 * 1024 * 1024,
+        )(left, tan_t, dmg_t, load_t)
+    asked, mech_total = lax.optimization_barrier((asked, mech_total))
     with jax.named_scope("source"):
         answer = call(
             functools.partial(source_kernel, cap),

time: 55.9 us -> 54.5 us (0.975)
  blocking collectives: 39.2 us -> 28.6 us
  waiting for transfers between devices: 1.3 us -> 4.73 us
  Pallas kernels: 9.86 us -> 13.1 us
  starting transfers between devices: 3.6 us -> 6.18 us
    all_to_all x3 -> x2, blocking collectives: 32.3 us -> 21.7 us  [swap(): return lax.all_to_all(x, axes, split_axis=0, concat_axis=0, tiled=True)]
    all_to_all x0 -> x1, waiting for transfers between devices: none -> 3.42 us  [swap(): return lax.all_to_all(x, axes, split_axis=0, concat_axis=0, tiled=True)]
    pallas_call x1 -> x2, Pallas kernels: 6.29 us -> 9.64 us  [the longest x1 5.41 us: on_device(): call(tangent_kernel, [sds((width, lanes)), sds((1, lanes))], 4, [pltpu.VM...]
    all_to_all x0 -> x1, starting transfers between devices: none -> 2.58 us  [swap(): return lax.all_to_all(x, axes, split_axis=0, concat_axis=0, tiled=True)]
  transfers between devices with their start and end apart: 2 -> 3, of which waited for: 1 -> 2; matrix products, arithmetic and copies ran while one was open for 0% -> 0% of each run, Pallas kernels for 0% -> 10%
where the time goes in v2:
time: 54.5 us; the launch traced here: 54.2 us
  blocking collectives  28.6 us (52%)
  Pallas kernels  13.1 us (24%)
  starting transfers between devices  6.18 us (11%)
  waiting for transfers between devices  4.73 us (9%)
  other arithmetic  0.83 us (2%)
  between operations  0.79 us (1%)
    all_to_all x2, blocking collectives, swap(): return lax.all_to_all(x, axes, split_axis=0, concat_axis=0, tiled=True)  21.7 us
    all_gather x1, blocking collectives, on_device(): group = lax.all_gather(fields, 'blk', axis=0, tiled=False)  6.87 us
    pallas_call x1, Pallas kernels, on_device(): call(tangent_kernel, [sds((width, lanes)), sds((1, lanes))], 4, [pltpu.VM...  5.41 us
    pallas_call x1, Pallas kernels, on_device(): call(functools.partial(laplacian_kernel, cap), [sds(parcel_shape(devices,...  4.23 us
    ppermute x1, starting transfers between devices, on_device(): mine_ghost = lax.ppermute(picked, both, hop)  3.6 us
    all_to_all x1, waiting for transfers between devices, swap(): return lax.all_to_all(x, axes, split_axis=0, concat_axis=0, tiled=True)  3.42 us
    all_to_all x1, starting transfers between devices, swap(): return lax.all_to_all(x, axes, split_axis=0, concat_axis=0, tiled=True)  2.58 us
    pallas_call x1, Pallas kernels, on_device(): call(functools.partial(source_kernel, cap), sds(parcel_shape(devices, cap...  1.85 us
  transfers between devices with their start and end apart: 3, of which 2 were waited for; matrix products, arithmetic and copies ran while one was open for 0% of the time, Pallas kernels for 10%

profile of v2, /device:TPU:0, one launch (start us, length us, event | category | flops | bytes accessed | tf_op | source)
XLA Modules:
  0.0 54.2 jit_solution(9945382161103297472)
XLA Ops:
  0.6 0.8 %pad_maximum_fusion.stacked = f32[192,128]{1,0:T(8,128)S(1)} fusion(f32[96,128]{1,0:T(8,128)} %bitcast.18, f32[96,128]{1,0:T(8,128)} %bitcast.16), kind=kLoop, calls=%fused_computation | loop fusion | flops 24576 | bytes 196608 | tf_op jit(solution)/shard_map/concatenate | solution.py:312
  1.5 6.9 %all-gather = bf16[768,128]{1,0:T(8,128)(2,1)S(1)} all-gather(bf16[192,128]{1,0:T(8,128)(2,1)S(1)} %fields.1), channel_id=2, replica_groups=mesh['dom'=8,'blk'=4] {'blk'}, dimensions={0}, use_global_device_ids=true | all-gather | bytes 245760 | tf_op jit(solution)/shard_map/all_gather | solution.py:315
  8.4 0.0 copy-done.7
  8.4 0.2 picks.1
  8.6 3.6 %collective-permute-start = (bf16[192,256]{1,0:T(8,128)(2,1)S(1)}, bf16[192,256]{1,0:T(8,128)(2,1)S(1)}, u32[]{:S(2)}, u32[]{:S(2)}) collective-permute-start(bf16[192,256]{1,0:T(8,128)(2,1)S(1)} %picks.1), channel_id=1, source_target_pairs={{0,4},{2,6},{4,8},{5,1},{6,10},{7,3},{8,12},{9,5},{10,14},{11,7},{... | collective-permute-start | bytes 294920 | tf_op jit(solution)/shard_map/ppermute | solution.py:334
  12.2 0.0 copy-done.8
  12.2 0.0 copy-start
  12.2 0.0 copy-start.1
  12.2 0.0 copy-start.2
  12.2 0.0 copy-start.6
  12.3 0.3 requests.1
  12.5 11.9 %all_to_all.15.request = f32[32,1,128]{2,1,0:T(1,128)S(1)} all-to-all(f32[32,1,128]{2,1,0:T(1,128)S(1)} %get-tuple-element.20), channel_id=1, replica_groups=mesh['dom'=8,'blk'=4] {'dom','blk'}, dimensions={0} | all-to-all | bytes 32768 | tf_op jit(solution)/shard_map/all_to_all | solution.py:280
  24.4 0.0 collective-permute-done.mine_ghost
  24.4 0.0 collective-permute-start.1
  24.4 1.3 %collective-permute-done.1.other_ghost = bf16[192,256]{1,0:T(8,128)(2,1)S(1)} collective-permute-done((bf16[192,256]{1,0:T(8,128)(2,1)S(1)}, bf16[192,256]{1,0:T(8,128)(2,1)S(1)}, u32[]{:S(2)}, u32[]{:S(2)}) %collective-permute-start.1) | collective-permute-done | bytes 98336 | tf_op jit(solution)/shard_map/ppermute | solution.py:336
  25.7 0.0 copy-done
  25.7 0.0 copy-done.1
  25.7 0.0 copy-done.2
  25.7 0.0 copy-done.6
  25.7 0.0 copy-start.5
  25.7 4.2 %laplacian.1 = (f32[32,3,4,128]{3,2,1,0:T(4,128)}, bf16[128,480]{1,0:T(8,128)(2,1)S(1)}) custom-call(bf16[4,192,128]{2,1,0:T(8,128)(2,1)S(1)} %bitcast.15, bf16[192,256]{1,0:T(8,128)(2,1)S(1)} %collective-permute-done.mine_ghost, bf16[192,256]{1,0:T(8,128)(2,1)S(1)} %collective-permute-done.1.other_ghost, s32[5,128]{1,0:T(8,128)S(1)} %bitcast.24, ...), custom_call_target="tpu_custom_call" | custom-call | flops 10000000000 | tf_op jit(solution)/shard_map/laplacian/pallas_call | solution.py:338
  30.0 2.6 %all-to-all-start.1 = ((f32[32,3,4,128]{3,2,1,0:T(4,128)}), f32[32,3,4,128]{3,2,1,0:T(4,128)S(1)}, u32[]{:S(2)}, u32[]{:S(2)}) async-start(f32[32,3,4,128]{3,2,1,0:T(4,128)} %get-tuple-element.23), calls=%async_computation.1 | async-start | bytes 393216 | tf_op jit(solution)/shard_map/all_to_all | solution.py:280
  32.6 0.0 copy-done.5
  32.6 0.0 copy-start.3
  32.6 0.0 copy-start.4
  32.6 0.0 copy-start.9
  32.6 5.4 %tangent.1 = (f32[96,128]{1,0:T(8,128)S(1)}, f32[1,128]{1,0:T(1,128)S(1)}) custom-call(bf16[128,480]{1,0:T(8,128)(2,1)S(1)} %get-tuple-element.24.left, bf16[5,96,96,128]{3,2,1,0:T(8,128)(2,1)} %bitcast.28, f32[96,128]{1,0:T(8,128)S(1)} %bitcast.20, f32[96,128]{1,0:T(8,128)S(1)} %bitcast.23), custom_call_target="tpu_custom_call" | custom-call | flops 10000000000 | tf_op jit(solution)/shard_map/tangent/pallas_call | solution.py:350
  38.0 3.4 %all-to-all-done.1.got = f32[32,3,4,128]{3,2,1,0:T(4,128)S(1)} async-done(((f32[32,3,4,128]{3,2,1,0:T(4,128)}), f32[32,3,4,128]{3,2,1,0:T(4,128)S(1)}, u32[]{:S(2)}, u32[]{:S(2)}) %all-to-all-start.1) | async-done | bytes 196640 | tf_op jit(solution)/shard_map/all_to_all | solution.py:280
  41.5 0.0 copy-done.4
  41.5 1.9 %source.1 = f32[32,1,4,128]{3,2,1,0:T(4,128)S(1)} custom-call(f32[32,3,4,128]{3,2,1,0:T(4,128)S(1)} %all-to-all-done.1.got, s32[1,128]{1,0:T(1,128)S(1)} %get-tuple-element.27.bucket, f32[27,96,128]{2,1,0:T(8,128)S(1)} %bitcast.22, f32[27,96,96]{2,1,0:T(8,128)S(1)} %copy-done.4, f32[1,27]{1,0:T(1,128)S(1)} %bitcast.27, f32[1,128]{1,0:T(1,128)S(1)} %get-tuple-element.28.mech_total), custom_call_target="tpu_custom_call" | custom-call | flops 10000000000 | tf_op jit(solution)/shard_map/source/pallas_call | solution.py:361
  43.3 9.8 %all_to_all.16.got = f32[32,1,4,128]{3,2,1,0:T(4,128)S(1)} all-to-all(f32[32,1,4,128]{3,2,1,0:T(4,128)S(1)} %source.1), channel_id=1, replica_groups=mesh['dom'=8,'blk'=4] {'dom','blk'}, dimensions={0} | all-to-all | bytes 131072 | tf_op jit(solution)/shard_map/all_to_all | solution.py:280
  53.1 1.1 %scale.1 = (f32[96,128]{1,0:T(8,128)}, f32[96,128]{1,0:T(8,128)}, f32[1,2]{1,0:T(1,128)}) custom-call(f32[32,1,4,128]{3,2,1,0:T(4,128)S(1)} %all_to_all.16.got, f32[32,1,128]{2,1,0:T(1,128)S(1)} %all_to_all.15.request, f32[96,128]{1,0:T(8,128)S(1)} %get-tuple-element.29.mech), custom_call_target="tpu_custom_call" | custom-call | tf_op jit(solution)/shard_map/scale/pallas_call | solution.py:370
  (5 shorter events, 0.0 us)
Async XLA Ops:
  1.5 6.9 %copy-start.7 = (s32[1,2,256]{2,1,0:T(2,128)S(1)}, s32[1,2,256]{2,1,0:T(2,128)}, u32[]{:S(2)}) copy-start(s32[1,2,256]{2,1,0:T(2,128)} %param.17) | copy-start | bytes 6148
  8.4 3.8 %copy-start.8 = (s32[128]{0:T(128)S(1)}, s32[128]{0:T(128)}, u32[]{:S(2)}) copy-start(s32[128]{0:T(128)} %param.19) | copy-start | bytes 1540
  8.6 15.8 %collective-permute-start = (bf16[192,256]{1,0:T(8,128)(2,1)S(1)}, bf16[192,256]{1,0:T(8,128)(2,1)S(1)}, u32[]{:S(2)}, u32[]{:S(2)}) collective-permute-start(bf16[192,256]{1,0:T(8,128)(2,1)S(1)} %picks.1), channel_id=1, source_target_pairs={{0,4},{2,6},{4,8},{5,1},{6,10},{7,3},{8,12},{9,5},{10,14},{11,7},{... | collective-permute-start | bytes 294920 | tf_op jit(solution)/shard_map/ppermute | solution.py:334
  12.2 13.5 %copy-start = (f32[128,96]{0,1:T(8,128)S(1)}, f32[128,96]{0,1:T(8,128)}, u32[]{:S(2)}) copy-start(f32[128,96]{0,1:T(8,128)} %param.11) | copy-start | bytes 147460
  12.2 13.5 %copy-start.1 = (f32[128,96]{0,1:T(8,128)S(1)}, f32[128,96]{0,1:T(8,128)}, u32[]{:S(2)}) copy-start(f32[128,96]{0,1:T(8,128)} %param.12) | copy-start | bytes 147460
  12.2 13.5 %copy-start.2 = (bf16[128,5,96,96]{0,3,2,1:T(8,128)(2,1)S(1)}, bf16[128,5,96,96]{0,3,2,1:T(8,128)(2,1)}, u32[]{:S(2)}) copy-start(bf16[128,5,96,96]{0,3,2,1:T(8,128)(2,1)} %param.15) | copy-start | bytes 35389444
  12.2 13.5 %copy-start.6 = (s32[128,5]{0,1:T(8,128)S(1)}, s32[128,5]{0,1:T(8,128)}, u32[]{:S(2)}) copy-start(s32[128,5]{0,1:T(8,128)} %param.16) | copy-start | bytes 7684
  24.4 1.3 %collective-permute-start.1 = (bf16[192,256]{1,0:T(8,128)(2,1)S(1)}, bf16[192,256]{1,0:T(8,128)(2,1)S(1)}, u32[]{:S(2)}, u32[]{:S(2)}) collective-permute-start(bf16[192,256]{1,0:T(8,128)(2,1)S(1)} %collective-permute-done.mine_ghost), channel_id=1, source_target_pairs={{0,1},{1,0},{2,3},{3,2},{4,5},{5,4},{6,7},{7,6},{8,9},{9,8},{10,11... | collective-permute-start | bytes 294920 | tf_op jit(solution)/shard_map/ppermute | solution.py:336
  25.7 6.8 %copy-start.5 = (f32[128,96]{0,1:T(8,128)S(1)}, f32[128,96]{0,1:T(8,128)}, u32[]{:S(2)}) copy-start(f32[128,96]{0,1:T(8,128)} %param.13) | copy-start | bytes 147460
  30.0 11.5 %all-to-all-start.1 = ((f32[32,3,4,128]{3,2,1,0:T(4,128)}), f32[32,3,4,128]{3,2,1,0:T(4,128)S(1)}, u32[]{:S(2)}, u32[]{:S(2)}) async-start(f32[32,3,4,128]{3,2,1,0:T(4,128)} %get-tuple-element.23), calls=%async_computation.1 | async-start | bytes 393216 | tf_op jit(solution)/shard_map/all_to_all | solution.py:280
  32.6 8.9 %copy-start.3 = (f32[128,27,96]{0,2,1:T(8,128)S(1)}, f32[128,27,96]{0,2,1:T(8,128)}, u32[]{:S(2)}) copy-start(f32[128,27,96]{0,2,1:T(8,128)} %param.18) | copy-start | bytes 3981316
  32.6 8.9 %copy-start.4 = (f32[27,96,96]{2,1,0:T(8,128)S(1)}, f32[27,96,96]{2,1,0:T(8,128)}, u32[]{:S(2)}) copy-start(f32[27,96,96]{2,1,0:T(8,128)} %smat.1) | copy-start | bytes 2985988
  32.6 8.9 %copy-start.9 = (f32[27]{0:T(128)S(1)}, f32[27]{0:T(128)}, u32[]{:S(2)}) copy-start(f32[27]{0:T(128)} %param.21) | copy-start | bytes 328

commit v3 on v2

--- a/solution.py
+++ b/solution.py
@@ -43,32 +43,37 @@
     return lax.broadcasted_iota(jnp.int32, shape, dim)
 
 
-def parcel_shape(devices, values, lanes):
-    return (devices, -(-values // (4 * lanes)), 4, lanes)
-
-
-def pack(hot, table, out, tail=0.0):
-    devices, groups, _, lanes = out.shape
+def section_size(values, lanes):
+    return -(-values // (4 * lanes))
+
+
+def pack(hot, table, out, section, tail=0.0):
+    devices, _, _, lanes = out.shape
     hi, lo = split2(table)
     moved = dot_nt(hot, hi) + dot_nt(hot, lo)
     cap, width = moved.shape[0] // devices, moved.shape[1]
+    first, size = section
     rows = [moved[k * devices : (k + 1) * devices] for k in range(cap)]
-    rows.append(jnp.zeros((devices, groups * 4 * lanes - cap * width), F32))
+    rows.append(jnp.zeros((devices, size * 4 * lanes - cap * width), F32))
     flat = jnp.concatenate(rows, axis=1)
-    for j in range(groups * 4):
+    for j in range(size * 4):
         line = flat[:, j * lanes : (j + 1) * lanes]
-        out[:, j // 4, j % 4, :] = line + tail if j == groups * 4 - 1 else line
-
-
-def unpack(hot, got, width):
-    devices, groups, _, lanes = got.shape
-    flat = jnp.concatenate([got[:, j // 4, j % 4, :] for j in range(groups * 4)], axis=1)
+        out[:, first + j // 4, j % 4, :] = line + tail if j == size * 4 - 1 else line
+
+
+def unpack(hot, got, width, sections):
+    devices, _, _, lanes = got.shape
     cap = hot.shape[0] // devices
-    rows = jnp.concatenate([flat[:, k * width : (k + 1) * width] for k in range(cap)], axis=0)
     blank = jnp.zeros((cap * devices, -width % lanes), F32)
-    tall = jnp.concatenate([rows, blank], axis=1).T[:width]
-    hi, lo = split2(tall)
-    return dot(hi, hot) + dot(lo, hot)
+    tall = []
+    for first, size in sections:
+        lines = [got[:, first + j // 4, j % 4, :] for j in range(size * 4)]
+        flat = jnp.concatenate(lines, axis=1)
+        rows = [flat[:, k * width : (k + 1) * width] for k in range(cap)]
+        tall.append(jnp.concatenate([jnp.concatenate(rows, axis=0), blank], axis=1).T[:width])
+    hi, lo = split2(jnp.concatenate(tall, axis=0))
+    found = dot(hi, hot) + dot(lo, hot)
+    return [found[i * width : (i + 1) * width] for i in range(len(sections))]
 
 
 def asked_hot(request, cap):
@@ -130,9 +135,10 @@
 def source_kernel(cap, got, bucket, hist, smat, weight, mech_total, out):
     quads, width, lanes = hist.shape
     hot = asking_hot(bucket, cap, got.shape[0])
-    held = unpack(hot, got, 3 * width)
+    size = got.shape[1] // 3
+    disp, v, u = unpack(hot, got, width, [(i * size, size) for i in range(3)])
     gap = jnp.zeros((lanes - width, lanes), F32)
-    d_hi, d_lo = split2(jnp.concatenate([held[:width], gap], axis=0))
+    d_hi, d_lo = split2(jnp.concatenate([disp, gap], axis=0))
     upper = jnp.concatenate([d_hi, d_lo], axis=1)
     lower = jnp.concatenate([d_hi, jnp.zeros_like(d_hi)], axis=1)
     sides = jnp.concatenate([upper, lower], axis=0)
@@ -143,52 +149,70 @@
         full = dot(jnp.concatenate(halves, axis=1), sides)
         strain = full[:, :lanes] + full[:, lanes:]
         acc = acc + weight[0, q] * jnp.maximum(hist[q], 0.5 * strain * strain)
-    dmg_res = held[width : 2 * width] + 2.0 * acc * held[2 * width :]
+    dmg_res = u + 2.0 * acc * v
     spare = iota((1, lanes), 1) - (lanes - 2)
     tail = jnp.where(spare == 0, mech_total[...], 0.0)
     tail = jnp.where(spare == 1, total_of(dmg_res), tail)
-    pack(hot, dmg_res, out, tail)
+    pack(hot, dmg_res, out, (0, out.shape[1]), tail)
+
+
+def columns_row(columns):
+    return jnp.concatenate([columns[k : k + 1, :] for k in range(columns.shape[0])], axis=1)
+
+
+def own_gather(group, rows, wanted):
+    table = jnp.concatenate([group[j, rows, :] for j in range(group.shape[0])], axis=1)
+    hot = one_hot(iota((table.shape[1], wanted.shape[1]), 0) == wanted)
+    return dot(table, hot)
+
+
+def ghost_gather(own, mine_ghost, other_ghost, rows, wanted):
+    ghost = mine_ghost.shape[1]
+    odd = lax.axis_index("blk") % 2
+    table = jnp.concatenate([mine_ghost[rows, :], other_ghost[rows, :]], axis=1)
+    hots = [
+        one_hot(iota((ghost, wanted.shape[1]), 0) + start == wanted)
+        for start in (own + odd * ghost, own + ghost - odd * ghost)
+    ]
+    return dot(table, jnp.concatenate(hots, axis=0))
+
+
+def stacked_columns(found, kblk):
+    lanes = found.shape[1] // kblk
+    cut = [found[:, k * lanes : (k + 1) * lanes] for k in range(kblk)]
+    return jnp.concatenate(cut, axis=0)
+
+
+def early_kernel(cap, group, columns, request, disp, damage, found, sections):
+    width = disp.shape[0]
+    found[...] = own_gather(group, pl.ds(width, width), columns_row(columns))
+    hot = asked_hot(request, cap)
+    size = sections.shape[1] // 2
+    pack(hot, disp[...], sections, (0, size))
+    pack(hot, damage[...] - 1.0, sections, (size, size))
 
 
 def laplacian_kernel(
     cap,
-    group,
+    found_own,
     mine_ghost,
     other_ghost,
     columns,
     lap,
     request,
-    disp,
     damage,
+    sections,
     parcels,
-    left,
     near,
     diff,
 ):
     kblk, rows, width, lanes = lap.shape
-    parts = group.shape[0]
-    ghost = mine_ghost.shape[1]
-    table = jnp.concatenate(
-        [group[j] for j in range(parts)] + [mine_ghost[...], other_ghost[...]], axis=1
+    own = lax.axis_size("blk") * lanes
+    half = pl.ds(width, width)
+    found = found_own[...] + ghost_gather(
+        own, mine_ghost, other_ghost, half, columns_row(columns)
     )
-    wanted = jnp.concatenate([columns[k : k + 1, :] for k in range(kblk)], axis=1)
-    odd = lax.axis_index("blk") % 2
-    own = parts * lanes
-    starts = (0, own + odd * ghost, own + ghost - odd * ghost)
-    hots = [
-        one_hot(iota((size, kblk * lanes), 0) + start == wanted)
-        for size, start in zip((own, ghost, ghost), starts)
-    ]
-    found = dot(table, jnp.concatenate(hots, axis=0))
-    tall = []
-    for field in range(2):
-        cut = [
-            found[field * width : (field + 1) * width, k * lanes : (k + 1) * lanes]
-            for k in range(kblk)
-        ]
-        tall.append(jnp.concatenate(cut, axis=0))
-    left[...] = tall[0].T.astype(BF16)
-    near[...] = tall[1]
+    near[...] = stacked_columns(found, kblk)
 
     @pl.loop(0, rows // 8)
     def _(step):
@@ -204,12 +228,14 @@
         sums = [jnp.sum(a, axis=0, keepdims=True) for a in acc]
         diff[pl.ds(pl.multiple_of(step * 8, 8), 8), :] = jnp.concatenate(sums, axis=0)
 
-    d = damage[...]
-    values = jnp.concatenate([disp[...], diff[...] + d, d - 1.0], axis=0)
-    pack(asked_hot(request, cap), values, parcels)
-
-
-def tangent_kernel(left, tan_hbm, damage, load, mech, mech_total, tan, sems):
+    size = sections.shape[1] // 2
+    parcels[:, : 2 * size, :, :] = sections[...]
+    pack(asked_hot(request, cap), diff[...] + damage[...], parcels, (2 * size, size))
+
+
+def tangent_kernel(
+    group, mine_ghost, other_ghost, columns, tan_hbm, damage, load, mech, mech_total, tan, left_ref, sems
+):
     kblk, rows, width, lanes = tan.shape
     depth = kblk * width
     steps = rows // 8
@@ -222,6 +248,12 @@
     def _(step):
         piece(step).start()
 
+    wanted = columns_row(columns)
+    own = group.shape[0] * lanes
+    half = pl.ds(0, width)
+    found = own_gather(group, half, wanted)
+    found = found + ghost_gather(own, mine_ghost, other_ghost, half, wanted)
+    left_ref[...] = stacked_columns(found, kblk).T.astype(BF16)
     lane = iota((8, 2 * lanes), 1) % lanes
     mine = iota((8, 2 * lanes), 0) == lane % 8
 
@@ -231,7 +263,7 @@
         lines = []
         for r in range(0, 8, 2):
             pair = [tan[:, step * 8 + r + j].reshape(depth, lanes) for j in range(2)]
-            full = dot(left[...], jnp.concatenate(pair, axis=1))
+            full = dot(left_ref[...], jnp.concatenate(pair, axis=1))
             kept = full[:8]
             for g in range(1, lanes // 8):
                 kept = jnp.where(lane // 8 == g, full[g * 8 : g * 8 + 8], kept)
@@ -250,7 +282,8 @@
     total = jnp.sum(last, axis=0, keepdims=True)[:, lanes - 2 :]
     norm = jnp.sqrt(total / entries + 1e-06)
     mech_out[...] = mech[...] / norm[:, 0:1]
-    dmg_out[...] = unpack(asked_hot(request, cap), got, width) / norm[:, 1:2]
+    (dmg,) = unpack(asked_hot(request, cap), got, width, [(0, got.shape[1])])
+    dmg_out[...] = dmg / norm[:, 1:2]
     norms[...] = norm
 
 
@@ -334,33 +367,41 @@
     mine_ghost = lax.ppermute(picked, both, hop)
     mine_ghost, wanted = lax.optimization_barrier((mine_ghost, wanted))
     other_ghost = lax.ppermute(mine_ghost, "blk", side)
+    size = section_size(cap * width, lanes)
+    with jax.named_scope("early"):
+        found, sections = call(
+            functools.partial(early_kernel, cap),
+            [sds((width, kblk * lanes)), sds((devices, 2 * size, 4, lanes))],
+            5,
+        )(group, cols_t, wanted, disp_t, dmg_t)
     with jax.named_scope("laplacian"):
-        parcels, left = call(
+        parcels = call(
             functools.partial(laplacian_kernel, cap),
-            [
-                sds(parcel_shape(devices, 3 * cap * width, lanes)),
-                sds((lanes, kblk * width), BF16),
-            ],
+            sds((devices, 3 * size, 4, lanes)),
             8,
             [pltpu.VMEM((kblk * width, lanes), F32), pltpu.VMEM((width, lanes), F32)],
             flops=FILL,
-        )(group, mine_ghost, other_ghost, cols_t, lap_t, wanted, disp_t, dmg_t)
+        )(found, mine_ghost, other_ghost, cols_t, lap_t, wanted, dmg_t, sections)
     asked = swap(parcels, both)
     with jax.named_scope("tangent"):
         mech, mech_total = call(
             tangent_kernel,
             [sds((width, lanes)), sds((1, lanes))],
-            4,
-            [pltpu.VMEM(tan_t.shape, BF16), pltpu.SemaphoreType.DMA((width // 8,))],
+            7,
+            [
+                pltpu.VMEM(tan_t.shape, BF16),
+                pltpu.VMEM((lanes, kblk * width), BF16),
+                pltpu.SemaphoreType.DMA((width // 8,)),
+            ],
             flops=FILL,
-            specs=[VM, ANY, VM, VM],
+            specs=[VM, VM, VM, VM, ANY, VM, VM],
             limit=48 * 1024 * 1024,
-        )(left, tan_t, dmg_t, load_t)
+        )(group, mine_ghost, other_ghost, cols_t, tan_t, dmg_t, load_t)
     asked, mech_total = lax.optimization_barrier((asked, mech_total))
     with jax.named_scope("source"):
         answer = call(
             functools.partial(source_kernel, cap),
-            sds(parcel_shape(devices, cap * width + 2, lanes)),
+            sds((devices, section_size(cap * width + 2, lanes), 4, lanes)),
             6,
             flops=FILL,
             specs=[VM, VM, VM, VM, SM, VM],

time: 54.5 us -> 54.1 us (level)
    ppermute x1, waiting for transfers between devices: 1.3 us -> 0.71 us  [on_device(): other_ghost = lax.ppermute(mine_ghost, 'blk', side)]
    pallas_call x3 -> x4, Pallas kernels: 11.5 us -> 11.6 us  [the longest x1 5.35 us: on_device(): call(tangent_kernel, [sds((width, lanes)), sds((1, lanes))], 7, [pltpu.VM...]
  transfers between devices with their start and end apart: 3 -> 3, of which waited for: 2 -> 2; matrix products, arithmetic and copies ran while one was open for 0% -> 0% of each run, Pallas kernels for 10% -> 11%
where the time goes in v3:
time: 54.1 us; the launch traced here: 53.8 us
  blocking collectives  28.6 us (53%)
  Pallas kernels  13.2 us (24%)
  starting transfers between devices  6.18 us (11%)
  waiting for transfers between devices  4.2 us (8%)
  other arithmetic  0.83 us (2%)
  between operations  0.79 us (1%)
    all_to_all x2, blocking collectives, swap(): return lax.all_to_all(x, axes, split_axis=0, concat_axis=0, tiled=True)  21.7 us
    all_gather x1, blocking collectives, on_device(): group = lax.all_gather(fields, 'blk', axis=0, tiled=False)  6.87 us
    pallas_call x1, Pallas kernels, on_device(): call(tangent_kernel, [sds((width, lanes)), sds((1, lanes))], 7, [pltpu.VM...  5.35 us
    pallas_call x1, Pallas kernels, on_device(): call(functools.partial(laplacian_kernel, cap), sds((devices, 3 * size, 4,...  3.75 us
    ppermute x1, starting transfers between devices, on_device(): mine_ghost = lax.ppermute(picked, both, hop)  3.6 us
    all_to_all x1, waiting for transfers between devices, swap(): return lax.all_to_all(x, axes, split_axis=0, concat_axis=0, tiled=True)  3.49 us
    all_to_all x1, starting transfers between devices, swap(): return lax.all_to_all(x, axes, split_axis=0, concat_axis=0, tiled=True)  2.58 us
    pallas_call x1, Pallas kernels, on_device(): call(functools.partial(source_kernel, cap), sds((devices, section_size(ca...  1.91 us
  transfers between devices with their start and end apart: 3, of which 2 were waited for; matrix products, arithmetic and copies ran while one was open for 0% of the time, Pallas kernels for 11%

profile of v3, /device:TPU:0, one launch (start us, length us, event | category | flops | bytes accessed | tf_op | source)
XLA Modules:
  0.0 53.8 jit_solution(16028293884708964308)
XLA Ops:
  0.6 0.8 %pad_maximum_fusion.stacked = f32[192,128]{1,0:T(8,128)S(1)} fusion(f32[96,128]{1,0:T(8,128)} %bitcast.19, f32[96,128]{1,0:T(8,128)} %bitcast.17), kind=kLoop, calls=%fused_computation | loop fusion | flops 24576 | bytes 196608 | tf_op jit(solution)/shard_map/concatenate | solution.py:345
  1.5 6.9 %all-gather = bf16[768,128]{1,0:T(8,128)(2,1)S(1)} all-gather(bf16[192,128]{1,0:T(8,128)(2,1)S(1)} %fields.1), channel_id=2, replica_groups=mesh['dom'=8,'blk'=4] {'blk'}, dimensions={0}, use_global_device_ids=true | all-gather | bytes 245760 | tf_op jit(solution)/shard_map/all_gather | solution.py:348
  8.4 0.0 copy-done.7
  8.4 0.2 picks.1
  8.6 3.6 %collective-permute-start = (bf16[192,256]{1,0:T(8,128)(2,1)S(1)}, bf16[192,256]{1,0:T(8,128)(2,1)S(1)}, u32[]{:S(2)}, u32[]{:S(2)}) collective-permute-start(bf16[192,256]{1,0:T(8,128)(2,1)S(1)} %picks.1), channel_id=1, source_target_pairs={{0,4},{2,6},{4,8},{5,1},{6,10},{7,3},{8,12},{9,5},{10,14},{11,7},{... | collective-permute-start | bytes 294920 | tf_op jit(solution)/shard_map/ppermute | solution.py:367
  12.2 0.0 copy-done.8
  12.2 0.0 copy-start
  12.2 0.0 copy-start.1
  12.2 0.0 copy-start.2
  12.2 0.0 copy-start.3
  12.3 0.3 requests.1
  12.5 11.9 %all_to_all.15.request = f32[32,1,128]{2,1,0:T(1,128)S(1)} all-to-all(f32[32,1,128]{2,1,0:T(1,128)S(1)} %get-tuple-element.20), channel_id=1, replica_groups=mesh['dom'=8,'blk'=4] {'dom','blk'}, dimensions={0} | all-to-all | bytes 32768 | tf_op jit(solution)/shard_map/all_to_all | solution.py:313
  24.4 0.0 collective-permute-done.mine_ghost
  24.4 0.0 collective-permute-start.1
  24.4 0.0 copy-done
  24.4 0.0 copy-done.1
  24.4 0.0 copy-done.2
  24.4 0.6 %early.1 = (f32[96,640]{1,0:T(8,128)S(1)}, f32[32,2,4,128]{3,2,1,0:T(4,128)S(1)}) custom-call(bf16[4,192,128]{2,1,0:T(8,128)(2,1)S(1)} %bitcast.15, s32[5,128]{1,0:T(8,128)S(1)} %bitcast.23, f32[32,1,128]{2,1,0:T(1,128)S(1)} %all_to_all.15.request, f32[96,128]{1,0:T(8,128)S(1)} %bitcast.18, f32[96,128]{1,0:T(8,128)S(1)} %bitcast.20), custom_call_target="tpu_custom_call" | custom-call | tf_op jit(solution)/shard_map/early/pallas_call | solution.py:372
  25.0 0.7 %collective-permute-done.1.other_ghost = bf16[192,256]{1,0:T(8,128)(2,1)S(1)} collective-permute-done((bf16[192,256]{1,0:T(8,128)(2,1)S(1)}, bf16[192,256]{1,0:T(8,128)(2,1)S(1)}, u32[]{:S(2)}, u32[]{:S(2)}) %collective-permute-start.1) | collective-permute-done | bytes 98336 | tf_op jit(solution)/shard_map/ppermute | solution.py:369
  25.7 0.0 copy-done.3
  25.7 3.8 %laplacian.1 = f32[32,3,4,128]{3,2,1,0:T(4,128)} custom-call(f32[96,640]{1,0:T(8,128)S(1)} %get-tuple-element.22.found_own, bf16[192,256]{1,0:T(8,128)(2,1)S(1)} %collective-permute-done.mine_ghost, bf16[192,256]{1,0:T(8,128)(2,1)S(1)} %collective-permute-done.1.other_ghost, s32[5,128]{1,0:T(8,128)S(1)} %bitcast.24, bf16[5,96,96,128]{3,2,1,0:T(8,128)(2,1)S(1)} %bitcast.26, ...), custom_call_target="tpu_custom_call" | custom-call | flops 10000000000 | tf_op jit(solution)/shard_map/laplacian/pallas_call | solution.py:378
  29.5 2.6 %all-to-all-start.1 = ((f32[32,3,4,128]{3,2,1,0:T(4,128)}), f32[32,3,4,128]{3,2,1,0:T(4,128)S(1)}, u32[]{:S(2)}, u32[]{:S(2)}) async-start(f32[32,3,4,128]{3,2,1,0:T(4,128)} %laplacian.1), calls=%async_computation.1 | async-start | bytes 393216 | tf_op jit(solution)/shard_map/all_to_all | solution.py:313
  32.1 0.0 copy-done.6
  32.1 0.0 copy-start.4
  32.1 0.0 copy-start.5
  32.1 0.0 copy-start.9
  32.1 5.3 %tangent.1 = (f32[96,128]{1,0:T(8,128)S(1)}, f32[1,128]{1,0:T(1,128)S(1)}) custom-call(bf16[4,192,128]{2,1,0:T(8,128)(2,1)S(1)} %bitcast.16, bf16[192,256]{1,0:T(8,128)(2,1)S(1)} %collective-permute-done.mine_ghost, bf16[192,256]{1,0:T(8,128)(2,1)S(1)} %collective-permute-done.1.other_ghost, s32[5,128]{1,0:T(8,128)S(1)} %bitcast.25, ...), custom_call_target="tpu_custom_call" | custom-call | flops 10000000000 | tf_op jit(solution)/shard_map/tangent/pallas_call | solution.py:387
  37.5 3.5 %all-to-all-done.1.got = f32[32,3,4,128]{3,2,1,0:T(4,128)S(1)} async-done(((f32[32,3,4,128]{3,2,1,0:T(4,128)}), f32[32,3,4,128]{3,2,1,0:T(4,128)S(1)}, u32[]{:S(2)}, u32[]{:S(2)}) %all-to-all-start.1) | async-done | bytes 196640 | tf_op jit(solution)/shard_map/all_to_all | solution.py:313
  41.0 0.0 copy-done.5
  41.0 1.9 %source.1 = f32[32,1,4,128]{3,2,1,0:T(4,128)S(1)} custom-call(f32[32,3,4,128]{3,2,1,0:T(4,128)S(1)} %all-to-all-done.1.got, s32[1,128]{1,0:T(1,128)S(1)} %get-tuple-element.27.bucket, f32[27,96,128]{2,1,0:T(8,128)S(1)} %bitcast.27, f32[27,96,96]{2,1,0:T(8,128)S(1)} %copy-done.5, f32[1,27]{1,0:T(1,128)S(1)} %bitcast.31, f32[1,128]{1,0:T(1,128)S(1)} %get-tuple-element.28.mech_total), custom_call_target="tpu_custom_call" | custom-call | flops 10000000000 | tf_op jit(solution)/shard_map/source/pallas_call | solution.py:402
  42.9 9.8 %all_to_all.16.got = f32[32,1,4,128]{3,2,1,0:T(4,128)S(1)} all-to-all(f32[32,1,4,128]{3,2,1,0:T(4,128)S(1)} %source.1), channel_id=1, replica_groups=mesh['dom'=8,'blk'=4] {'dom','blk'}, dimensions={0} | all-to-all | bytes 131072 | tf_op jit(solution)/shard_map/all_to_all | solution.py:313
  52.7 1.1 %scale.1 = (f32[96,128]{1,0:T(8,128)}, f32[96,128]{1,0:T(8,128)}, f32[1,2]{1,0:T(1,128)}) custom-call(f32[32,1,4,128]{3,2,1,0:T(4,128)S(1)} %all_to_all.16.got, f32[32,1,128]{2,1,0:T(1,128)S(1)} %all_to_all.15.request, f32[96,128]{1,0:T(8,128)S(1)} %get-tuple-element.29.mech), custom_call_target="tpu_custom_call" | custom-call | tf_op jit(solution)/shard_map/scale/pallas_call | solution.py:411
  (6 shorter events, 0.0 us)
Async XLA Ops:
  1.5 6.9 %copy-start.7 = (s32[1,2,256]{2,1,0:T(2,128)S(1)}, s32[1,2,256]{2,1,0:T(2,128)}, u32[]{:S(2)}) copy-start(s32[1,2,256]{2,1,0:T(2,128)} %param.17) | copy-start | bytes 6148
  8.4 3.8 %copy-start.8 = (s32[128]{0:T(128)S(1)}, s32[128]{0:T(128)}, u32[]{:S(2)}) copy-start(s32[128]{0:T(128)} %param.19) | copy-start | bytes 1540
  8.6 15.8 %collective-permute-start = (bf16[192,256]{1,0:T(8,128)(2,1)S(1)}, bf16[192,256]{1,0:T(8,128)(2,1)S(1)}, u32[]{:S(2)}, u32[]{:S(2)}) collective-permute-start(bf16[192,256]{1,0:T(8,128)(2,1)S(1)} %picks.1), channel_id=1, source_target_pairs={{0,4},{2,6},{4,8},{5,1},{6,10},{7,3},{8,12},{9,5},{10,14},{11,7},{... | collective-permute-start | bytes 294920 | tf_op jit(solution)/shard_map/ppermute | solution.py:367
  12.2 12.2 %copy-start = (f32[128,96]{0,1:T(8,128)S(1)}, f32[128,96]{0,1:T(8,128)}, u32[]{:S(2)}) copy-start(f32[128,96]{0,1:T(8,128)} %param.11) | copy-start | bytes 147460
  12.2 12.2 %copy-start.1 = (f32[128,96]{0,1:T(8,128)S(1)}, f32[128,96]{0,1:T(8,128)}, u32[]{:S(2)}) copy-start(f32[128,96]{0,1:T(8,128)} %param.12) | copy-start | bytes 147460
  12.2 12.2 %copy-start.2 = (s32[128,5]{0,1:T(8,128)S(1)}, s32[128,5]{0,1:T(8,128)}, u32[]{:S(2)}) copy-start(s32[128,5]{0,1:T(8,128)} %param.16) | copy-start | bytes 7684
  12.2 13.5 %copy-start.3 = (bf16[128,5,96,96]{0,3,2,1:T(8,128)(2,1)S(1)}, bf16[128,5,96,96]{0,3,2,1:T(8,128)(2,1)}, u32[]{:S(2)}) copy-start(bf16[128,5,96,96]{0,3,2,1:T(8,128)(2,1)} %param.15) | copy-start | bytes 35389444
  24.4 1.3 %collective-permute-start.1 = (bf16[192,256]{1,0:T(8,128)(2,1)S(1)}, bf16[192,256]{1,0:T(8,128)(2,1)S(1)}, u32[]{:S(2)}, u32[]{:S(2)}) collective-permute-start(bf16[192,256]{1,0:T(8,128)(2,1)S(1)} %collective-permute-done.mine_ghost), channel_id=1, source_target_pairs={{0,1},{1,0},{2,3},{3,2},{4,5},{5,4},{6,7},{7,6},{8,9},{9,8},{10,11... | collective-permute-start | bytes 294920 | tf_op jit(solution)/shard_map/ppermute | solution.py:369
  25.7 6.3 %copy-start.6 = (f32[128,96]{0,1:T(8,128)S(1)}, f32[128,96]{0,1:T(8,128)}, u32[]{:S(2)}) copy-start(f32[128,96]{0,1:T(8,128)} %param.13) | copy-start | bytes 147460
  29.5 11.5 %all-to-all-start.1 = ((f32[32,3,4,128]{3,2,1,0:T(4,128)}), f32[32,3,4,128]{3,2,1,0:T(4,128)S(1)}, u32[]{:S(2)}, u32[]{:S(2)}) async-start(f32[32,3,4,128]{3,2,1,0:T(4,128)} %laplacian.1), calls=%async_computation.1 | async-start | bytes 393216 | tf_op jit(solution)/shard_map/all_to_all | solution.py:313
  32.1 8.9 %copy-start.4 = (f32[128,27,96]{0,2,1:T(8,128)S(1)}, f32[128,27,96]{0,2,1:T(8,128)}, u32[]{:S(2)}) copy-start(f32[128,27,96]{0,2,1:T(8,128)} %param.18) | copy-start | bytes 3981316
  32.1 8.9 %copy-start.5 = (f32[27,96,96]{2,1,0:T(8,128)S(1)}, f32[27,96,96]{2,1,0:T(8,128)}, u32[]{:S(2)}) copy-start(f32[27,96,96]{2,1,0:T(8,128)} %smat.1) | copy-start | bytes 2985988
  32.1 8.9 %copy-start.9 = (f32[27]{0:T(128)S(1)}, f32[27]{0:T(128)}, u32[]{:S(2)}) copy-start(f32[27]{0:T(128)} %param.21) | copy-start | bytes 328

commit v4 on v3

--- a/solution.py
+++ b/solution.py
@@ -10,6 +10,8 @@
 F32 = jnp.float32
 BF16 = jnp.bfloat16
 FILL = 10**10
+POINTS = 9
+STEP = 16
 VMEM_LIMIT = 4 * 1024 * 1024
 
 
@@ -142,13 +144,18 @@
     upper = jnp.concatenate([d_hi, d_lo], axis=1)
     lower = jnp.concatenate([d_hi, jnp.zeros_like(d_hi)], axis=1)
     sides = jnp.concatenate([upper, lower], axis=0)
-    blank = jnp.zeros((width, lanes - width), F32)
     acc = jnp.zeros((width, lanes), F32)
-    for q in range(quads):
-        halves = split2(jnp.concatenate([smat[q], blank], axis=1))
+    for first in range(0, quads, POINTS):
+        points = range(first, min(first + POINTS, quads))
+        rows = smat[pl.ds(first, len(points))].reshape(len(points) * width, width)
+        blank = jnp.zeros((rows.shape[0], lanes - width), F32)
+        halves = split2(jnp.concatenate([rows, blank], axis=1))
         full = dot(jnp.concatenate(halves, axis=1), sides)
         strain = full[:, :lanes] + full[:, lanes:]
-        acc = acc + weight[0, q] * jnp.maximum(hist[q], 0.5 * strain * strain)
+        energy = 0.5 * strain * strain
+        for q in points:
+            part = energy[(q - first) * width : (q - first + 1) * width]
+            acc = acc + weight[0, q] * jnp.maximum(hist[q], part)
     dmg_res = u + 2.0 * acc * v
     spare = iota((1, lanes), 1) - (lanes - 2)
     tail = jnp.where(spare == 0, mech_total[...], 0.0)
@@ -183,23 +190,23 @@
     return jnp.concatenate(cut, axis=0)
 
 
-def early_kernel(cap, group, columns, request, disp, damage, found, sections):
+def early_kernel(cap, group, columns, request, disp, damage, found, sections, asked):
     width = disp.shape[0]
     found[...] = own_gather(group, pl.ds(width, width), columns_row(columns))
     hot = asked_hot(request, cap)
+    asked[...] = hot
     size = sections.shape[1] // 2
     pack(hot, disp[...], sections, (0, size))
     pack(hot, damage[...] - 1.0, sections, (size, size))
 
 
 def laplacian_kernel(
-    cap,
     found_own,
     mine_ghost,
     other_ghost,
     columns,
     lap,
-    request,
+    asked,
     damage,
     sections,
     parcels,
@@ -214,23 +221,24 @@
     )
     near[...] = stacked_columns(found, kblk)
 
-    @pl.loop(0, rows // 8)
+    @pl.loop(0, rows // STEP)
     def _(step):
-        acc = [jnp.zeros((8, lanes), F32) for _ in range(8)]
+        acc = [jnp.zeros((8, lanes), F32) for _ in range(STEP)]
         for k in range(kblk):
             for c in range(0, width, 16):
                 base = k * width + c
                 lo = near[base : base + 8, :]
                 hi = near[base + 8 : base + 16, :]
-                for r in range(8):
-                    block = lap[k, step * 8 + r, c : c + 16, :].astype(F32)
+                for r in range(STEP):
+                    block = lap[k, step * STEP + r, c : c + 16, :].astype(F32)
                     acc[r] = acc[r] + (block[:8] * lo + block[8:] * hi)
         sums = [jnp.sum(a, axis=0, keepdims=True) for a in acc]
-        diff[pl.ds(pl.multiple_of(step * 8, 8), 8), :] = jnp.concatenate(sums, axis=0)
+        place = pl.ds(pl.multiple_of(step * STEP, STEP), STEP)
+        diff[place, :] = jnp.concatenate(sums, axis=0)
 
     size = sections.shape[1] // 2
     parcels[:, : 2 * size, :, :] = sections[...]
-    pack(asked_hot(request, cap), diff[...] + damage[...], parcels, (2 * size, size))
+    pack(asked[...], diff[...] + damage[...], parcels, (2 * size, size))
 
 
 def tangent_kernel(
@@ -369,19 +377,23 @@
     other_ghost = lax.ppermute(mine_ghost, "blk", side)
     size = section_size(cap * width, lanes)
     with jax.named_scope("early"):
-        found, sections = call(
+        found, sections, asked_by = call(
             functools.partial(early_kernel, cap),
-            [sds((width, kblk * lanes)), sds((devices, 2 * size, 4, lanes))],
+            [
+                sds((width, kblk * lanes)),
+                sds((devices, 2 * size, 4, lanes)),
+                sds((cap * devices, lanes), BF16),
+            ],
             5,
         )(group, cols_t, wanted, disp_t, dmg_t)
     with jax.named_scope("laplacian"):
         parcels = call(
-            functools.partial(laplacian_kernel, cap),
+            laplacian_kernel,
             sds((devices, 3 * size, 4, lanes)),
             8,
             [pltpu.VMEM((kblk * width, lanes), F32), pltpu.VMEM((width, lanes), F32)],
             flops=FILL,
-        )(found, mine_ghost, other_ghost, cols_t, lap_t, wanted, dmg_t, sections)
+        )(found, mine_ghost, other_ghost, cols_t, lap_t, asked_by, dmg_t, sections)
     asked = swap(parcels, both)
     with jax.named_scope("tangent"):
         mech, mech_total = call(
@@ -405,6 +417,7 @@
             6,
             flops=FILL,
             specs=[VM, VM, VM, VM, SM, VM],
+            limit=3 * VMEM_LIMIT,
         )(asked, bucket, hist_t, strain_matrix, quad_weight[None, :], mech_total)
     got = swap(answer, both)
     with jax.named_scope("scale"):

time: 54.1 us -> 53.9 us (level)
  transfers between devices with their start and end apart: 3 -> 3, of which waited for: 2 -> 2; matrix products, arithmetic and copies ran while one was open for 0% -> 0% of each run, Pallas kernels for 11% -> 12%
where the time goes in v4:
time: 53.9 us; the launch traced here: 53.6 us
  blocking collectives  28.6 us (53%)
  Pallas kernels  13 us (24%)
  starting transfers between devices  6.18 us (11%)
  waiting for transfers between devices  4.19 us (8%)
  other arithmetic  0.83 us (2%)
  between operations  0.79 us (1%)
    all_to_all x2, blocking collectives, swap(): return lax.all_to_all(x, axes, split_axis=0, concat_axis=0, tiled=True)  21.7 us
    all_gather x1, blocking collectives, on_device(): group = lax.all_gather(fields, 'blk', axis=0, tiled=False)  6.87 us
    pallas_call x1, Pallas kernels, on_device(): call(tangent_kernel, [sds((width, lanes)), sds((1, lanes))], 7, [pltpu.VM...  5.34 us
    pallas_call x1, Pallas kernels, on_device(): call(laplacian_kernel, sds((devices, 3 * size, 4, lanes)), 8, [pltpu.VMEM...  3.61 us
    ppermute x1, starting transfers between devices, on_device(): mine_ghost = lax.ppermute(picked, both, hop)  3.6 us
    all_to_all x1, waiting for transfers between devices, swap(): return lax.all_to_all(x, axes, split_axis=0, concat_axis=0, tiled=True)  3.49 us
    all_to_all x1, starting transfers between devices, swap(): return lax.all_to_all(x, axes, split_axis=0, concat_axis=0, tiled=True)  2.58 us
    pallas_call x1, Pallas kernels, on_device(): call(functools.partial(source_kernel, cap), sds((devices, section_size(ca...  1.91 us
  transfers between devices with their start and end apart: 3, of which 2 were waited for; matrix products, arithmetic and copies ran while one was open for 0% of the time, Pallas kernels for 12%

profile of v4, /device:TPU:0, one launch (start us, length us, event | category | flops | bytes accessed | tf_op | source)
XLA Modules:
  0.0 53.6 jit_solution(1537430877157539674)
XLA Ops:
  0.6 0.8 %pad_maximum_fusion.stacked = f32[192,128]{1,0:T(8,128)S(1)} fusion(f32[96,128]{1,0:T(8,128)} %bitcast.19, f32[96,128]{1,0:T(8,128)} %bitcast.17), kind=kLoop, calls=%fused_computation | loop fusion | flops 24576 | bytes 196608 | tf_op jit(solution)/shard_map/concatenate | solution.py:353
  1.5 6.9 %all-gather = bf16[768,128]{1,0:T(8,128)(2,1)S(1)} all-gather(bf16[192,128]{1,0:T(8,128)(2,1)S(1)} %fields.1), channel_id=2, replica_groups=mesh['dom'=8,'blk'=4] {'blk'}, dimensions={0}, use_global_device_ids=true | all-gather | bytes 245760 | tf_op jit(solution)/shard_map/all_gather | solution.py:356
  8.4 0.0 copy-done.7
  8.4 0.2 picks.1
  8.6 3.6 %collective-permute-start = (bf16[192,256]{1,0:T(8,128)(2,1)S(1)}, bf16[192,256]{1,0:T(8,128)(2,1)S(1)}, u32[]{:S(2)}, u32[]{:S(2)}) collective-permute-start(bf16[192,256]{1,0:T(8,128)(2,1)S(1)} %picks.1), channel_id=1, source_target_pairs={{0,4},{2,6},{4,8},{5,1},{6,10},{7,3},{8,12},{9,5},{10,14},{11,7},{... | collective-permute-start | bytes 294920 | tf_op jit(solution)/shard_map/ppermute | solution.py:375
  12.2 0.0 copy-done.8
  12.2 0.0 copy-start
  12.2 0.0 copy-start.1
  12.2 0.0 copy-start.2
  12.2 0.0 copy-start.3
  12.3 0.3 requests.1
  12.5 11.9 %all_to_all.15.request = f32[32,1,128]{2,1,0:T(1,128)S(1)} all-to-all(f32[32,1,128]{2,1,0:T(1,128)S(1)} %get-tuple-element.21), channel_id=1, replica_groups=mesh['dom'=8,'blk'=4] {'dom','blk'}, dimensions={0} | all-to-all | bytes 32768 | tf_op jit(solution)/shard_map/all_to_all | solution.py:321
  24.4 0.0 collective-permute-done.mine_ghost
  24.4 0.0 collective-permute-start.1
  24.4 0.0 copy-done
  24.4 0.0 copy-done.1
  24.4 0.0 copy-done.2
  24.4 0.6 %early.1 = (f32[96,640]{1,0:T(8,128)S(1)}, f32[32,2,4,128]{3,2,1,0:T(4,128)S(1)}, bf16[160,128]{1,0:T(8,128)(2,1)S(1)}) custom-call(bf16[4,192,128]{2,1,0:T(8,128)(2,1)S(1)} %bitcast.15, s32[5,128]{1,0:T(8,128)S(1)} %bitcast.23, f32[32,1,128]{2,1,0:T(1,128)S(1)} %all_to_all.15.request, f32[96,128]{1,0:T(8,128)S(1)} %bitcast.18, f32[96,128]{1,0:T(8,128)S(1)} %bitcast.20), custom_call_target="tpu_custom_call" | custom-call | tf_op jit(solution)/shard_map/early/pallas_call | solution.py:380
  25.0 0.7 %collective-permute-done.1.other_ghost = bf16[192,256]{1,0:T(8,128)(2,1)S(1)} collective-permute-done((bf16[192,256]{1,0:T(8,128)(2,1)S(1)}, bf16[192,256]{1,0:T(8,128)(2,1)S(1)}, u32[]{:S(2)}, u32[]{:S(2)}) %collective-permute-start.1) | collective-permute-done | bytes 98336 | tf_op jit(solution)/shard_map/ppermute | solution.py:377
  25.7 0.0 copy-done.3
  25.7 3.6 %laplacian.1 = f32[32,3,4,128]{3,2,1,0:T(4,128)} custom-call(f32[96,640]{1,0:T(8,128)S(1)} %get-tuple-element.23.found_own, bf16[192,256]{1,0:T(8,128)(2,1)S(1)} %collective-permute-done.mine_ghost, bf16[192,256]{1,0:T(8,128)(2,1)S(1)} %collective-permute-done.1.other_ghost, s32[5,128]{1,0:T(8,128)S(1)} %bitcast.24, bf16[5,96,96,128]{3,2,1,0:T(8,128)(2,1)S(1)} %bitcast.26, ...), custom_call_target="tpu_custom_call" | custom-call | flops 10000000000 | tf_op jit(solution)/shard_map/laplacian/pallas_call | solution.py:390
  29.3 2.6 %all-to-all-start.1 = ((f32[32,3,4,128]{3,2,1,0:T(4,128)}), f32[32,3,4,128]{3,2,1,0:T(4,128)S(1)}, u32[]{:S(2)}, u32[]{:S(2)}) async-start(f32[32,3,4,128]{3,2,1,0:T(4,128)} %laplacian.1), calls=%async_computation.1 | async-start | bytes 393216 | tf_op jit(solution)/shard_map/all_to_all | solution.py:321
  31.9 0.0 copy-done.6
  31.9 0.0 copy-start.4
  31.9 0.0 copy-start.5
  31.9 0.0 copy-start.9
  32.0 5.3 %tangent.1 = (f32[96,128]{1,0:T(8,128)S(1)}, f32[1,128]{1,0:T(1,128)S(1)}) custom-call(bf16[4,192,128]{2,1,0:T(8,128)(2,1)S(1)} %bitcast.16, bf16[192,256]{1,0:T(8,128)(2,1)S(1)} %collective-permute-done.mine_ghost, bf16[192,256]{1,0:T(8,128)(2,1)S(1)} %collective-permute-done.1.other_ghost, s32[5,128]{1,0:T(8,128)S(1)} %bitcast.25, ...), custom_call_target="tpu_custom_call" | custom-call | flops 10000000000 | tf_op jit(solution)/shard_map/tangent/pallas_call | solution.py:399
  37.3 3.5 %all-to-all-done.1.got = f32[32,3,4,128]{3,2,1,0:T(4,128)S(1)} async-done(((f32[32,3,4,128]{3,2,1,0:T(4,128)}), f32[32,3,4,128]{3,2,1,0:T(4,128)S(1)}, u32[]{:S(2)}, u32[]{:S(2)}) %all-to-all-start.1) | async-done | bytes 196640 | tf_op jit(solution)/shard_map/all_to_all | solution.py:321
  40.8 0.0 copy-done.5
  40.8 1.9 %source.1 = f32[32,1,4,128]{3,2,1,0:T(4,128)S(1)} custom-call(f32[32,3,4,128]{3,2,1,0:T(4,128)S(1)} %all-to-all-done.1.got, s32[1,128]{1,0:T(1,128)S(1)} %get-tuple-element.29.bucket, f32[27,96,128]{2,1,0:T(8,128)S(1)} %bitcast.27, f32[27,96,96]{2,1,0:T(8,128)S(1)} %copy-done.5, f32[1,27]{1,0:T(1,128)S(1)} %bitcast.31, f32[1,128]{1,0:T(1,128)S(1)} %get-tuple-element.30.mech_total), custom_call_target="tpu_custom_call" | custom-call | flops 10000000000 | tf_op jit(solution)/shard_map/source/pallas_call | solution.py:414
  42.7 9.8 %all_to_all.16.got = f32[32,1,4,128]{3,2,1,0:T(4,128)S(1)} all-to-all(f32[32,1,4,128]{3,2,1,0:T(4,128)S(1)} %source.1), channel_id=1, replica_groups=mesh['dom'=8,'blk'=4] {'dom','blk'}, dimensions={0} | all-to-all | bytes 131072 | tf_op jit(solution)/shard_map/all_to_all | solution.py:321
  52.6 1.1 %scale.1 = (f32[96,128]{1,0:T(8,128)}, f32[96,128]{1,0:T(8,128)}, f32[1,2]{1,0:T(1,128)}) custom-call(f32[32,1,4,128]{3,2,1,0:T(4,128)S(1)} %all_to_all.16.got, f32[32,1,128]{2,1,0:T(1,128)S(1)} %all_to_all.15.request, f32[96,128]{1,0:T(8,128)S(1)} %get-tuple-element.31.mech), custom_call_target="tpu_custom_call" | custom-call | tf_op jit(solution)/shard_map/scale/pallas_call | solution.py:424
  (6 shorter events, 0.0 us)
Async XLA Ops:
  1.5 6.9 %copy-start.7 = (s32[1,2,256]{2,1,0:T(2,128)S(1)}, s32[1,2,256]{2,1,0:T(2,128)}, u32[]{:S(2)}) copy-start(s32[1,2,256]{2,1,0:T(2,128)} %param.17) | copy-start | bytes 6148
  8.4 3.8 %copy-start.8 = (s32[128]{0:T(128)S(1)}, s32[128]{0:T(128)}, u32[]{:S(2)}) copy-start(s32[128]{0:T(128)} %param.19) | copy-start | bytes 1540
  8.6 15.8 %collective-permute-start = (bf16[192,256]{1,0:T(8,128)(2,1)S(1)}, bf16[192,256]{1,0:T(8,128)(2,1)S(1)}, u32[]{:S(2)}, u32[]{:S(2)}) collective-permute-start(bf16[192,256]{1,0:T(8,128)(2,1)S(1)} %picks.1), channel_id=1, source_target_pairs={{0,4},{2,6},{4,8},{5,1},{6,10},{7,3},{8,12},{9,5},{10,14},{11,7},{... | collective-permute-start | bytes 294920 | tf_op jit(solution)/shard_map/ppermute | solution.py:375
  12.2 12.2 %copy-start = (f32[128,96]{0,1:T(8,128)S(1)}, f32[128,96]{0,1:T(8,128)}, u32[]{:S(2)}) copy-start(f32[128,96]{0,1:T(8,128)} %param.11) | copy-start | bytes 147460
  12.2 12.2 %copy-start.1 = (f32[128,96]{0,1:T(8,128)S(1)}, f32[128,96]{0,1:T(8,128)}, u32[]{:S(2)}) copy-start(f32[128,96]{0,1:T(8,128)} %param.12) | copy-start | bytes 147460
  12.2 12.2 %copy-start.2 = (s32[128,5]{0,1:T(8,128)S(1)}, s32[128,5]{0,1:T(8,128)}, u32[]{:S(2)}) copy-start(s32[128,5]{0,1:T(8,128)} %param.16) | copy-start | bytes 7684
  12.2 13.5 %copy-start.3 = (bf16[128,5,96,96]{0,3,2,1:T(8,128)(2,1)S(1)}, bf16[128,5,96,96]{0,3,2,1:T(8,128)(2,1)}, u32[]{:S(2)}) copy-start(bf16[128,5,96,96]{0,3,2,1:T(8,128)(2,1)} %param.15) | copy-start | bytes 35389444
  24.4 1.3 %collective-permute-start.1 = (bf16[192,256]{1,0:T(8,128)(2,1)S(1)}, bf16[192,256]{1,0:T(8,128)(2,1)S(1)}, u32[]{:S(2)}, u32[]{:S(2)}) collective-permute-start(bf16[192,256]{1,0:T(8,128)(2,1)S(1)} %collective-permute-done.mine_ghost), channel_id=1, source_target_pairs={{0,1},{1,0},{2,3},{3,2},{4,5},{5,4},{6,7},{7,6},{8,9},{9,8},{10,11... | collective-permute-start | bytes 294920 | tf_op jit(solution)/shard_map/ppermute | solution.py:377
  25.7 6.2 %copy-start.6 = (f32[128,96]{0,1:T(8,128)S(1)}, f32[128,96]{0,1:T(8,128)}, u32[]{:S(2)}) copy-start(f32[128,96]{0,1:T(8,128)} %param.13) | copy-start | bytes 147460
  29.3 11.5 %all-to-all-start.1 = ((f32[32,3,4,128]{3,2,1,0:T(4,128)}), f32[32,3,4,128]{3,2,1,0:T(4,128)S(1)}, u32[]{:S(2)}, u32[]{:S(2)}) async-start(f32[32,3,4,128]{3,2,1,0:T(4,128)} %laplacian.1), calls=%async_computation.1 | async-start | bytes 393216 | tf_op jit(solution)/shard_map/all_to_all | solution.py:321
  31.9 8.9 %copy-start.4 = (f32[128,27,96]{0,2,1:T(8,128)S(1)}, f32[128,27,96]{0,2,1:T(8,128)}, u32[]{:S(2)}) copy-start(f32[128,27,96]{0,2,1:T(8,128)} %param.18) | copy-start | bytes 3981316
  31.9 8.9 %copy-start.5 = (f32[27,96,96]{2,1,0:T(8,128)S(1)}, f32[27,96,96]{2,1,0:T(8,128)}, u32[]{:S(2)}) copy-start(f32[27,96,96]{2,1,0:T(8,128)} %smat.1) | copy-start | bytes 2985988
  31.9 8.9 %copy-start.9 = (f32[27]{0:T(128)S(1)}, f32[27]{0:T(128)}, u32[]{:S(2)}) copy-start(f32[27]{0:T(128)} %param.21) | copy-start | bytes 328

commit v5 on v4

--- a/solution.py
+++ b/solution.py
@@ -108,6 +108,8 @@
     d = dest[...]
     owner = d // lanes
     slot = d - owner * lanes
+    blocks = lax.axis_size("blk")
+    owner = owner % blocks * (devices // blocks) + owner // blocks
     square = jnp.broadcast_to(owner.astype(F32), (lanes, lanes))
     diag = iota((lanes, lanes), 0) == iota((lanes, lanes), 1)
     column = jnp.sum(jnp.where(diag, square, 0.0), axis=1, keepdims=True)
@@ -338,7 +340,7 @@
     kblk = tangent.shape[1]
     quads = hist_mech.shape[1]
     ghost = send_lists.shape[2]
-    both = ("dom", "blk")
+    both = ("blk", "dom")
     devices = lax.axis_size(both)
     groups = lax.axis_size("dom")
     disp_t = displacement.T
@@ -372,7 +374,7 @@
     hop = [(a * blocks + b, (a + 1 - b % 2 * 2) * blocks + b) for a, b in everyone]
     hop = [(i, j) for i, j in hop if 0 <= j < groups * blocks]
     side = [(b, b ^ 1) for b in range(blocks)]
-    mine_ghost = lax.ppermute(picked, both, hop)
+    mine_ghost = lax.ppermute(picked, ("dom", "blk"), hop)
     mine_ghost, wanted = lax.optimization_barrier((mine_ghost, wanted))
     other_ghost = lax.ppermute(mine_ghost, "blk", side)
     size = section_size(cap * width, lanes)

time: 53.9 us -> 53.8 us (level)
  no operation moved by 1% of the time
where the time goes in v5:
time: 53.8 us; the launch traced here: 53.5 us
  blocking collectives  28.8 us (54%)
  Pallas kernels  13 us (24%)
  starting transfers between devices  6.18 us (11%)
  waiting for transfers between devices  3.85 us (7%)
  other arithmetic  0.83 us (2%)
  between operations  0.79 us (1%)
    all_to_all x2, blocking collectives, swap(): return lax.all_to_all(x, axes, split_axis=0, concat_axis=0, tiled=True)  21.9 us
    all_gather x1, blocking collectives, on_device(): group = lax.all_gather(fields, 'blk', axis=0, tiled=False)  6.87 us
    pallas_call x1, Pallas kernels, on_device(): call(tangent_kernel, [sds((width, lanes)), sds((1, lanes))], 7, [pltpu.VM...  5.35 us
    pallas_call x1, Pallas kernels, on_device(): call(laplacian_kernel, sds((devices, 3 * size, 4, lanes)), 8, [pltpu.VMEM...  3.61 us
    ppermute x1, starting transfers between devices, on_device(): mine_ghost = lax.ppermute(picked, ('dom', 'blk'), hop)  3.6 us
    all_to_all x1, waiting for transfers between devices, swap(): return lax.all_to_all(x, axes, split_axis=0, concat_axis=0, tiled=True)  3.15 us
    all_to_all x1, starting transfers between devices, swap(): return lax.all_to_all(x, axes, split_axis=0, concat_axis=0, tiled=True)  2.58 us
    pallas_call x1, Pallas kernels, on_device(): call(functools.partial(source_kernel, cap), sds((devices, section_size(ca...  1.9 us
  transfers between devices with their start and end apart: 3, of which 2 were waited for; matrix products, arithmetic and copies ran while one was open for 0% of the time, Pallas kernels for 12%

profile of v5, /device:TPU:0, one launch (start us, length us, event | category | flops | bytes accessed | tf_op | source)
XLA Modules:
  0.0 53.5 jit_solution(11722815739625680393)
XLA Ops:
  0.6 0.8 %pad_maximum_fusion.stacked = f32[192,128]{1,0:T(8,128)S(1)} fusion(f32[96,128]{1,0:T(8,128)} %bitcast.19, f32[96,128]{1,0:T(8,128)} %bitcast.17), kind=kLoop, calls=%fused_computation | loop fusion | flops 24576 | bytes 196608 | tf_op jit(solution)/shard_map/concatenate | solution.py:355
  1.5 6.9 %all-gather = bf16[768,128]{1,0:T(8,128)(2,1)S(1)} all-gather(bf16[192,128]{1,0:T(8,128)(2,1)S(1)} %fields.1), channel_id=2, replica_groups=mesh['dom'=8,'blk'=4] {'blk'}, dimensions={0}, use_global_device_ids=true | all-gather | bytes 245760 | tf_op jit(solution)/shard_map/all_gather | solution.py:358
  8.4 0.0 copy-done.7
  8.4 0.2 picks.1
  8.6 3.6 %collective-permute-start = (bf16[192,256]{1,0:T(8,128)(2,1)S(1)}, bf16[192,256]{1,0:T(8,128)(2,1)S(1)}, u32[]{:S(2)}, u32[]{:S(2)}) collective-permute-start(bf16[192,256]{1,0:T(8,128)(2,1)S(1)} %picks.1), channel_id=1, source_target_pairs={{0,4},{2,6},{4,8},{5,1},{6,10},{7,3},{8,12},{9,5},{10,14},{11,7},{... | collective-permute-start | bytes 294920 | tf_op jit(solution)/shard_map/ppermute | solution.py:377
  12.2 0.0 copy-done.8
  12.2 0.0 copy-start
  12.2 0.0 copy-start.1
  12.2 0.0 copy-start.2
  12.2 0.0 copy-start.3
  12.3 0.3 requests.1
  12.5 11.8 %all_to_all.15.request = f32[32,1,128]{2,1,0:T(1,128)S(1)} all-to-all(f32[32,1,128]{2,1,0:T(1,128)S(1)} %get-tuple-element.21), channel_id=1, replica_groups=mesh['dom'=8,'blk'=4] {'blk','dom'}, dimensions={0} | all-to-all | bytes 32768 | tf_op jit(solution)/shard_map/all_to_all | solution.py:323
  24.4 0.0 collective-permute-done.mine_ghost
  24.4 0.0 collective-permute-start.1
  24.4 0.0 copy-done
  24.4 0.0 copy-done.1
  24.4 0.0 copy-done.2
  24.4 0.6 %early.1 = (f32[96,640]{1,0:T(8,128)S(1)}, f32[32,2,4,128]{3,2,1,0:T(4,128)S(1)}, bf16[160,128]{1,0:T(8,128)(2,1)S(1)}) custom-call(bf16[4,192,128]{2,1,0:T(8,128)(2,1)S(1)} %bitcast.15, s32[5,128]{1,0:T(8,128)S(1)} %bitcast.23, f32[32,1,128]{2,1,0:T(1,128)S(1)} %all_to_all.15.request, f32[96,128]{1,0:T(8,128)S(1)} %bitcast.18, f32[96,128]{1,0:T(8,128)S(1)} %bitcast.20), custom_call_target="tpu_custom_call" | custom-call | tf_op jit(solution)/shard_map/early/pallas_call | solution.py:382
  25.0 0.7 %collective-permute-done.1.other_ghost = bf16[192,256]{1,0:T(8,128)(2,1)S(1)} collective-permute-done((bf16[192,256]{1,0:T(8,128)(2,1)S(1)}, bf16[192,256]{1,0:T(8,128)(2,1)S(1)}, u32[]{:S(2)}, u32[]{:S(2)}) %collective-permute-start.1) | collective-permute-done | bytes 98336 | tf_op jit(solution)/shard_map/ppermute | solution.py:379
  25.7 0.0 copy-done.3
  25.7 3.6 %laplacian.1 = f32[32,3,4,128]{3,2,1,0:T(4,128)} custom-call(f32[96,640]{1,0:T(8,128)S(1)} %get-tuple-element.23.found_own, bf16[192,256]{1,0:T(8,128)(2,1)S(1)} %collective-permute-done.mine_ghost, bf16[192,256]{1,0:T(8,128)(2,1)S(1)} %collective-permute-done.1.other_ghost, s32[5,128]{1,0:T(8,128)S(1)} %bitcast.24, bf16[5,96,96,128]{3,2,1,0:T(8,128)(2,1)S(1)} %bitcast.26, ...), custom_call_target="tpu_custom_call" | custom-call | flops 10000000000 | tf_op jit(solution)/shard_map/laplacian/pallas_call | solution.py:392
  29.3 2.6 %all-to-all-start.1 = ((f32[32,3,4,128]{3,2,1,0:T(4,128)}), f32[32,3,4,128]{3,2,1,0:T(4,128)S(1)}, u32[]{:S(2)}, u32[]{:S(2)}) async-start(f32[32,3,4,128]{3,2,1,0:T(4,128)} %laplacian.1), calls=%async_computation.1 | async-start | bytes 393216 | tf_op jit(solution)/shard_map/all_to_all | solution.py:323
  31.9 0.0 copy-done.6
  31.9 0.0 copy-start.4
  31.9 0.0 copy-start.5
  31.9 0.0 copy-start.9
  31.9 5.3 %tangent.1 = (f32[96,128]{1,0:T(8,128)S(1)}, f32[1,128]{1,0:T(1,128)S(1)}) custom-call(bf16[4,192,128]{2,1,0:T(8,128)(2,1)S(1)} %bitcast.16, bf16[192,256]{1,0:T(8,128)(2,1)S(1)} %collective-permute-done.mine_ghost, bf16[192,256]{1,0:T(8,128)(2,1)S(1)} %collective-permute-done.1.other_ghost, s32[5,128]{1,0:T(8,128)S(1)} %bitcast.25, ...), custom_call_target="tpu_custom_call" | custom-call | flops 10000000000 | tf_op jit(solution)/shard_map/tangent/pallas_call | solution.py:401
  37.3 3.1 %all-to-all-done.1.got = f32[32,3,4,128]{3,2,1,0:T(4,128)S(1)} async-done(((f32[32,3,4,128]{3,2,1,0:T(4,128)}), f32[32,3,4,128]{3,2,1,0:T(4,128)S(1)}, u32[]{:S(2)}, u32[]{:S(2)}) %all-to-all-start.1) | async-done | bytes 196640 | tf_op jit(solution)/shard_map/all_to_all | solution.py:323
  40.4 0.0 copy-done.5
  40.5 1.9 %source.1 = f32[32,1,4,128]{3,2,1,0:T(4,128)S(1)} custom-call(f32[32,3,4,128]{3,2,1,0:T(4,128)S(1)} %all-to-all-done.1.got, s32[1,128]{1,0:T(1,128)S(1)} %get-tuple-element.29.bucket, f32[27,96,128]{2,1,0:T(8,128)S(1)} %bitcast.27, f32[27,96,96]{2,1,0:T(8,128)S(1)} %copy-done.5, f32[1,27]{1,0:T(1,128)S(1)} %bitcast.31, f32[1,128]{1,0:T(1,128)S(1)} %get-tuple-element.30.mech_total), custom_call_target="tpu_custom_call" | custom-call | flops 10000000000 | tf_op jit(solution)/shard_map/source/pallas_call | solution.py:416
  42.4 10.0 %all_to_all.16.got = f32[32,1,4,128]{3,2,1,0:T(4,128)S(1)} all-to-all(f32[32,1,4,128]{3,2,1,0:T(4,128)S(1)} %source.1), channel_id=1, replica_groups=mesh['dom'=8,'blk'=4] {'blk','dom'}, dimensions={0} | all-to-all | bytes 131072 | tf_op jit(solution)/shard_map/all_to_all | solution.py:323
  52.4 1.1 %scale.1 = (f32[96,128]{1,0:T(8,128)}, f32[96,128]{1,0:T(8,128)}, f32[1,2]{1,0:T(1,128)}) custom-call(f32[32,1,4,128]{3,2,1,0:T(4,128)S(1)} %all_to_all.16.got, f32[32,1,128]{2,1,0:T(1,128)S(1)} %all_to_all.15.request, f32[96,128]{1,0:T(8,128)S(1)} %get-tuple-element.31.mech), custom_call_target="tpu_custom_call" | custom-call | tf_op jit(solution)/shard_map/scale/pallas_call | solution.py:426
  (6 shorter events, 0.0 us)
Async XLA Ops:
  1.5 6.9 %copy-start.7 = (s32[1,2,256]{2,1,0:T(2,128)S(1)}, s32[1,2,256]{2,1,0:T(2,128)}, u32[]{:S(2)}) copy-start(s32[1,2,256]{2,1,0:T(2,128)} %param.17) | copy-start | bytes 6148
  8.4 3.8 %copy-start.8 = (s32[128]{0:T(128)S(1)}, s32[128]{0:T(128)}, u32[]{:S(2)}) copy-start(s32[128]{0:T(128)} %param.19) | copy-start | bytes 1540
  8.6 15.8 %collective-permute-start = (bf16[192,256]{1,0:T(8,128)(2,1)S(1)}, bf16[192,256]{1,0:T(8,128)(2,1)S(1)}, u32[]{:S(2)}, u32[]{:S(2)}) collective-permute-start(bf16[192,256]{1,0:T(8,128)(2,1)S(1)} %picks.1), channel_id=1, source_target_pairs={{0,4},{2,6},{4,8},{5,1},{6,10},{7,3},{8,12},{9,5},{10,14},{11,7},{... | collective-permute-start | bytes 294920 | tf_op jit(solution)/shard_map/ppermute | solution.py:377
  12.2 12.2 %copy-start = (f32[128,96]{0,1:T(8,128)S(1)}, f32[128,96]{0,1:T(8,128)}, u32[]{:S(2)}) copy-start(f32[128,96]{0,1:T(8,128)} %param.11) | copy-start | bytes 147460
  12.2 12.2 %copy-start.1 = (f32[128,96]{0,1:T(8,128)S(1)}, f32[128,96]{0,1:T(8,128)}, u32[]{:S(2)}) copy-start(f32[128,96]{0,1:T(8,128)} %param.12) | copy-start | bytes 147460
  12.2 12.2 %copy-start.2 = (s32[128,5]{0,1:T(8,128)S(1)}, s32[128,5]{0,1:T(8,128)}, u32[]{:S(2)}) copy-start(s32[128,5]{0,1:T(8,128)} %param.16) | copy-start | bytes 7684
  12.2 13.5 %copy-start.3 = (bf16[128,5,96,96]{0,3,2,1:T(8,128)(2,1)S(1)}, bf16[128,5,96,96]{0,3,2,1:T(8,128)(2,1)}, u32[]{:S(2)}) copy-start(bf16[128,5,96,96]{0,3,2,1:T(8,128)(2,1)} %param.15) | copy-start | bytes 35389444
  24.4 1.3 %collective-permute-start.1 = (bf16[192,256]{1,0:T(8,128)(2,1)S(1)}, bf16[192,256]{1,0:T(8,128)(2,1)S(1)}, u32[]{:S(2)}, u32[]{:S(2)}) collective-permute-start(bf16[192,256]{1,0:T(8,128)(2,1)S(1)} %collective-permute-done.mine_ghost), channel_id=1, source_target_pairs={{0,1},{1,0},{2,3},{3,2},{4,5},{5,4},{6,7},{7,6},{8,9},{9,8},{10,11... | collective-permute-start | bytes 294920 | tf_op jit(solution)/shard_map/ppermute | solution.py:379
  25.7 6.2 %copy-start.6 = (f32[128,96]{0,1:T(8,128)S(1)}, f32[128,96]{0,1:T(8,128)}, u32[]{:S(2)}) copy-start(f32[128,96]{0,1:T(8,128)} %param.13) | copy-start | bytes 147460
  29.3 11.1 %all-to-all-start.1 = ((f32[32,3,4,128]{3,2,1,0:T(4,128)}), f32[32,3,4,128]{3,2,1,0:T(4,128)S(1)}, u32[]{:S(2)}, u32[]{:S(2)}) async-start(f32[32,3,4,128]{3,2,1,0:T(4,128)} %laplacian.1), calls=%async_computation.1 | async-start | bytes 393216 | tf_op jit(solution)/shard_map/all_to_all | solution.py:323
  31.9 8.5 %copy-start.4 = (f32[128,27,96]{0,2,1:T(8,128)S(1)}, f32[128,27,96]{0,2,1:T(8,128)}, u32[]{:S(2)}) copy-start(f32[128,27,96]{0,2,1:T(8,128)} %param.18) | copy-start | bytes 3981316
  31.9 8.5 %copy-start.5 = (f32[27,96,96]{2,1,0:T(8,128)S(1)}, f32[27,96,96]{2,1,0:T(8,128)}, u32[]{:S(2)}) copy-start(f32[27,96,96]{2,1,0:T(8,128)} %smat.1) | copy-start | bytes 2985988
  31.9 8.5 %copy-start.9 = (f32[27]{0:T(128)S(1)}, f32[27]{0:T(128)}, u32[]{:S(2)}) copy-start(f32[27]{0:T(128)} %param.21) | copy-start | bytes 328
